TPU v7x, 32 devices: a whole 2x2x4 slice. The times are simulated.
32 devices in a mesh: dp: 8 (over y, x, core), tensor: 4 (over z).
Axes of the slice: x: 2, y: 2, z: 4, core: 2. Of those that a mesh axis runs over, the one named last changes fastest.
Arguments:
- pixels: bfloat16 [25600, 768], P(('dp', 'tensor')), may hold values from -6 to 6
- crop_sides: int32 [256], P(('dp', 'tensor')), may hold values from 7 to 10, as said below
- out_cotangent: bfloat16 [25600, 768], P(('dp', 'tensor')), may hold values from -6 to 6
- depth_kernel: bfloat16 [49, 768], replicated, may hold values from -0.875 to 0.875
- depth_bias: bfloat16 [768], replicated, may hold values from -1.5 to 1.5
- norm_gain: bfloat16 [768], replicated, may hold values from 0.099609375 to 1.8984375
- norm_shift: bfloat16 [768], replicated, may hold values from -1.5 to 1.5
- expand_weight: bfloat16 [768, 3072], P(None, 'tensor'), may hold values from -0.21875 to 0.21875
- expand_bias: bfloat16 [3072], P('tensor'), may hold values from -1.5 to 1.5
- reduce_weight: bfloat16 [3072, 768], P('tensor'), may hold values from -0.109375 to 0.109375
- reduce_bias: bfloat16 [768], replicated, may hold values from -1.5 to 1.5
- layer_scale: bfloat16 [768], replicated, may hold values from 0.5 to 2
Outputs:
- block_out: bfloat16 [25600, 768], P(('dp', 'tensor'))
- input_grad: float32 [25600, 768], P(('dp', 'tensor'))
- kernel_grad: float32 [49, 768], replicated
- depth_bias_grad: float32 [768], replicated
- gain_grad: float32 [768], replicated
- shift_grad: float32 [768], replicated
- expand_grad: float32 [768, 3072], P(None, 'tensor')
- expand_bias_grad: float32 [3072], P('tensor')
- reduce_grad: float32 [3072, 768], P('tensor')
- reduce_bias_grad: float32 [768], replicated
- scale_grad: float32 [768], replicated
Inputs may be any that keep to these rules, and one draw needn't show every extreme that they name: `crop_sides`: each image's crop side is 7, 8 or 10; image 0 has 10 and image 1 has 7.
All inputs are finite; a program needn't handle non-finite values.
Results may differ from a plain program's by a relative error of at most 0.0066.
Values may be sent and summed in bfloat16 or wider, within the bound.
A program may use at most 320 MiB of HBM per device.

v0:
```python
import jax
import jax.numpy as jnp
from jax import lax
from jax.sharding import PartitionSpec as P

KERNEL = 7
SIDE = 10


norm_eps = 1e-06


def pixel_mask(crop_sides):
    places = jnp.arange(SIDE * SIDE, dtype=jnp.int32)
    row_index = places // SIDE
    col_index = places % SIDE
    inside = (row_index[None, :] < crop_sides[:, None]) & (col_index[None, :] < crop_sides[:, None])
    return inside.astype(jnp.float32).reshape(-1, 1)


def front_part(values, keep_mask, kernel, bias, gain, shift):
    width = values.shape[1]
    images = (values * keep_mask).reshape(-1, SIDE, SIDE, width)
    margin = KERNEL // 2
    padded = jnp.pad(images, ((0, 0), (margin, margin), (margin, margin), (0, 0)))
    mixed = jnp.zeros_like(images)
    for offset_row in range(KERNEL):
        for offset_col in range(KERNEL):
            window = padded[:, offset_row : offset_row + SIDE, offset_col : offset_col + SIDE, :]
            mixed = mixed + window * kernel[offset_row * KERNEL + offset_col]
    mixed = (mixed + bias).reshape(values.shape)
    center = jnp.mean(mixed, axis=1, keepdims=True)
    deviation = mixed - center
    spread = jnp.mean(deviation * deviation, axis=1, keepdims=True)
    return deviation * lax.rsqrt(spread + norm_eps) * gain + shift


def contract_rows(left_side, right_side):
    return lax.dot_general(
        left_side, right_side, (((0,), (0,)), ((), ())), preferred_element_type=jnp.float32
    )


def contract_cols(left_side, right_side):
    return lax.dot_general(
        left_side, right_side, (((1,), (1,)), ((), ())), preferred_element_type=jnp.float32
    )


def gelu_exact(value):
    return jax.nn.gelu(value, approximate=False)


def per_device(
    pixels,
    crop_sides,
    out_cotangent,
    depth_kernel,
    depth_bias,
    norm_gain,
    norm_shift,
    expand_weight,
    expand_bias,
    reduce_weight,
    reduce_bias,
    layer_scale,
):
    keep_mask = pixel_mask(crop_sides)
    pixels_wide = pixels.astype(jnp.float32)

    def front_only(values, kernel, bias, gain, shift):
        return front_part(values, keep_mask, kernel, bias, gain, shift)

    normed_wide, front_back = jax.vjp(
        front_only,
        pixels_wide,
        depth_kernel.astype(jnp.float32),
        depth_bias.astype(jnp.float32),
        norm_gain.astype(jnp.float32),
        norm_shift.astype(jnp.float32),
    )
    normed = normed_wide.astype(jnp.bfloat16)
    scale_wide = layer_scale.astype(jnp.float32)
    reduce_bias_wide = reduce_bias.astype(jnp.float32)
    cot_masked = out_cotangent.astype(jnp.float32) * keep_mask
    branch_cot = (scale_wide * cot_masked).astype(jnp.bfloat16)
    hidden = jnp.dot(
        lax.all_gather(normed, "tensor", axis=0, tiled=True),
        expand_weight,
        preferred_element_type=jnp.float32,
    ) + expand_bias.astype(jnp.float32)
    active = gelu_exact(hidden).astype(jnp.bfloat16)
    branch = (
        lax.psum_scatter(
            jnp.dot(active, reduce_weight, preferred_element_type=jnp.float32),
            "tensor",
            scatter_dimension=0,
            tiled=True,
        )
        + reduce_bias_wide
    )
    cot_group = lax.all_gather(branch_cot, "tensor", axis=0, tiled=True)
    reduce_grad = contract_rows(active, cot_group)
    active_cot = contract_cols(cot_group, reduce_weight)
    hidden_cot = jax.vjp(gelu_exact, hidden)[1](active_cot)[0].astype(jnp.bfloat16)
    expand_grad = contract_rows(lax.all_gather(normed, "tensor", axis=0, tiled=True), hidden_cot)
    normed_cot = lax.psum_scatter(
        contract_cols(hidden_cot, expand_weight), "tensor", scatter_dimension=0, tiled=True
    )
    expand_bias_grad = jnp.sum(hidden_cot.astype(jnp.float32), axis=0)
    block_out = (keep_mask * (pixels_wide + scale_wide * branch)).astype(jnp.bfloat16)
    pixel_cot, kernel_grad, depth_bias_grad, gain_grad, shift_grad = front_back(normed_cot)
    input_grad = pixel_cot + cot_masked
    scale_grad = jnp.sum(cot_masked * branch, axis=0)
    reduce_bias_grad = jnp.sum(branch_cot.astype(jnp.float32), axis=0)
    expand_grad, expand_bias_grad, reduce_grad = lax.psum(
        (expand_grad, expand_bias_grad, reduce_grad), "dp"
    )
    kernel_grad, depth_bias_grad, gain_grad, shift_grad, reduce_bias_grad, scale_grad = lax.psum(
        (kernel_grad, depth_bias_grad, gain_grad, shift_grad, reduce_bias_grad, scale_grad),
        ("dp", "tensor"),
    )
    return (
        block_out,
        input_grad,
        kernel_grad,
        depth_bias_grad,
        gain_grad,
        shift_grad,
        expand_grad,
        expand_bias_grad,
        reduce_grad,
        reduce_bias_grad,
        scale_grad,
    )


def solution(mesh):
    in_specs = (
        P(("dp", "tensor"), None),
        P(("dp", "tensor")),
        P(("dp", "tensor"), None),
        P(),
        P(),
        P(),
        P(),
        P(None, "tensor"),
        P("tensor"),
        P("tensor", None),
        P(),
        P(),
    )
    out_specs = (
        P(("dp", "tensor"), None),
        P(("dp", "tensor"), None),
        P(),
        P(),
        P(),
        P(),
        P(None, "tensor"),
        P("tensor"),
        P("tensor", None),
        P(),
        P(),
    )
    return jax.shard_map(
        per_device, mesh=mesh, in_specs=in_specs, out_specs=out_specs, check_vma=False
    )
```

profile of v0, /device:TPU:0, one launch (start us, length us, event | category | flops | bytes accessed | tf_op | source)
XLA Modules:
  0.0 1044.4 jit_solution(28303449401991202)
XLA Ops:
  7.3 1.0 convert_element_type.64
  8.2 0.7 slice_reduce_fusion.46
  9.0 0.7 slice_reduce_fusion.47
  9.8 0.7 slice_reduce_fusion.48
  10.6 0.7 and_convert_fusion
  11.4 1.3 convert_element_type.63
  12.7 0.7 convert_element_type.65
  13.4 4.7 convert_reduce_fusion.1
  18.0 4.1 reshape.391
  22.5 91.9 %fusion.11 = (f32[8,10,10]{2,1,0:T(8,128)S(1)}, f32[8,10,10,768]{3,2,1,0:T(8,128)}) fusion(f32[768]{0:T(1024)S(1)} %convert_element_type.65, f32[768]{0:T(1024)S(1)} %get-tuple-element.65, f32[768]{0:T(1024)S(1)} %get-tuple-element.66, f32[768]{0:T(1024)} %get-tuple-element.67, f32[768]{0:T(1024)} %get-tuple-element.68, f32[768]{0:T(1024)} %get-tuple-element.69, ...), kind=kLoop, calls=%fused_computation.249 | loop fusion | flops 60824800 | bytes 5072000 | tf_op jit(solution)/shard_map/jvp()/reduce_sum | solution.py:32
  114.6 2.7 multiply_reduce_fusion.48
  117.4 4.4 reshape.392
  122.0 3.3 add_convert_fusion.1
  125.4 0.7 all-gather.5.cloned.1.call-update
  126.6 94.2 %all-gather.3.cloned.1.call-done = bf16[3200,768]{1,0:T(8,128)(2,1)} async-done(((bf16[800,768]{1,0:T(8,128)(2,1)}), bf16[3200,768]{1,0:T(8,128)(2,1)}) %all-gather.3.cloned.1.call-update) | async-done | bytes 4915216 | tf_op jit(solution)/shard_map/all_gather | solution.py:88
  220.8 8.8 fusion.12
  229.7 84.4 %all-gather.5.cloned.1.call-done = bf16[3200,768]{1,0:T(8,128)(2,1)} async-done(((bf16[800,768]{1,0:T(8,128)(2,1)}), bf16[3200,768]{1,0:T(8,128)(2,1)}) %all-gather.5.cloned.1.call-update) | async-done | bytes 4915216 | tf_op jit(solution)/shard_map/all_gather | solution.py:102
  314.1 28.8 %convert_reduce_fusion = (f32[768]{0:T(1024)S(1)}, bf16[3200,768]{1,0:T(8,128)(2,1)S(1)}, f32[3200,768]{1,0:T(8,128)}) fusion(f32[3200,768]{1,0:T(8,128)} %fusion.12, f32[768]{0:T(1024)S(1)} %convert_element_type.69, bf16[3200,768]{1,0:T(8,128)(2,1)} %all-gather.5.cloned.1.call-done, bf16[768,768]{1,0:T(8,128)(2,1)S(1)} %copy-done), kind=kOutput, calls=%fused_computation.50 | convolution fusion | flops 3959192832 | bytes 30676992 | tf_op jit(solution)/shard_map/dot_general | solution.py:45
  342.9 2.2 copy-done.90
  345.1 6.6 fusion.14
  351.7 11.2 %multiply_convert_fusion = bf16[3200,768]{1,0:T(8,128)(2,1)} fusion(f32[3200,768]{1,0:T(8,128)} %get-tuple-element.123, f32[3200,768]{1,0:T(8,128)} %fusion.12, f32[768]{0:T(1024)S(1)} %convert_element_type.69), kind=kLoop, calls=%fused_computation.52 | loop fusion | flops 9830400 | bytes 24579072 | tf_op jit(solution)/shard_map/convert_element_type | solution.py:92
  363.0 8.8 fusion.13
  371.9 0.6 copy-done.88
  372.5 14.9 %psum.68 = f32[768]{0:T(1024)} all-reduce(f32[768]{0:T(1024)S(1)} %get-tuple-element.121), channel_id=1, replica_groups=mesh['dp'=8,'tensor'=4] {'dp'}, use_global_device_ids=true, to_apply=%region_64.65 | all-reduce | flops 768 | bytes 6144 | tf_op jit(solution)/shard_map/psum | solution.py:116
  387.4 9.8 fusion.15
  397.2 8.0 fusion.16
  405.3 112.5 %reduce-scatter.5.cloned.1.call-done = f32[800,768]{1,0:T(8,128)} async-done(((f32[3200,768]{1,0:T(8,128)}), f32[800,768]{1,0:T(8,128)}) %reduce-scatter.5.cloned.1.call-update) | async-done | bytes 2457616 | tf_op jit(solution)/shard_map/reduce_scatter | solution.py:107
  517.8 3.5 multiply_reduce_fusion.50
  521.3 4.0 fusion.10
  525.4 163.3 %reduce-scatter.3.cloned.1.call-done = f32[800,768]{1,0:T(8,128)} async-done(((f32[3200,768]{1,0:T(8,128)}), f32[800,768]{1,0:T(8,128)}) %reduce-scatter.3.cloned.1.call-update) | async-done | bytes 2457616 | tf_op jit(solution)/shard_map/reduce_scatter | solution.py:94
  688.6 5.0 fusion.8
  693.6 4.1 reshape.393
  697.8 31.5 %multiply_reduce_fusion.46 = (f32[768]{0:T(1024)S(1)}, f32[768]{0:T(1024)S(1)}, f32[768]{0:T(1024)S(1)}, f32[768]{0:T(1024)S(1)}, f32[768]{0:T(1024)S(1)}, /*ind...) fusion(f32[8,10,10,768]{3,2,1,0:T(8,128)} %reshape.393, ...), kind=kLoop, calls=%fused_computation.119 | loop fusion | flops 22104576 | bytes 4970496 | tf_op jit(solution)/shard_map/transpose(jvp())/reduce_sum | solution.py:30
  729.3 26.3 %multiply_reduce_fusion.47 = (f32[768]{0:T(1024)S(1)}, f32[768]{0:T(1024)S(1)}, f32[768]{0:T(1024)S(1)}, f32[768]{0:T(1024)S(1)}, f32[768]{0:T(1024)S(1)}, /*ind...) fusion(f32[8,10,10,768]{3,2,1,0:T(8,128)} %reshape.393, ...), kind=kLoop, calls=%fused_computation.120 | loop fusion | flops 22104576 | bytes 4970496 | tf_op jit(solution)/shard_map/transpose(jvp())/reduce_sum | solution.py:30
  755.6 24.7 %multiply_reduce_fusion.45 = (f32[768]{0:T(1024)S(1)}, f32[768]{0:T(1024)S(1)}, f32[768]{0:T(1024)S(1)}, f32[768]{0:T(1024)S(1)}, f32[768]{0:T(1024)S(1)}, /*ind...) fusion(f32[8,10,10,768]{3,2,1,0:T(8,128)} %reshape.393, ...), kind=kLoop, calls=%fused_computation.118 | loop fusion | flops 18422784 | bytes 19716096 | tf_op jit(solution)/shard_map/transpose(jvp())/reduce_sum | solution.py:30
  780.5 10.2 broadcast_multiply_fusion.2
  791.0 22.8 %broadcast_multiply_fusion.1 = (f32[8,10,10,768]{3,2,1,0:T(8,128)}, f32[8,10,10,768]{3,2,1,0:T(8,128)}, f32[8,10,10,768]{3,2,1,0:T(8,128)}, f32[8,10,10,768]{3,2...) fusion(f32[8,10,10,768]{3,2,1,0:T(8,128)S(1)} %copy-done.2, ...), kind=kLoop, calls=%fused_computation.138 | loop fusion | flops 11059200 | bytes 46749696 | tf_op jit(solution)/shard_map/transpose(jvp())/mul | solution.py:30
  814.0 22.5 %broadcast_multiply_fusion = (f32[8,10,10,768]{3,2,1,0:T(8,128)}, f32[8,10,10,768]{3,2,1,0:T(8,128)}, f32[8,10,10,768]{3,2,1,0:T(8,128)}, f32[8,10,10,768]{3,2,1...) fusion(f32[8,10,10,768]{3,2,1,0:T(8,128)S(1)} %copy-done.2, ...), kind=kLoop, calls=%fused_computation.137 | loop fusion | flops 11059200 | bytes 46749696 | tf_op jit(solution)/shard_map/transpose(jvp())/mul | solution.py:30
  837.0 55.4 %pad_add_fusion = f32[8,16,16,768]{3,2,1,0:T(8,128)} fusion(f32[8,10,10,768]{3,2,1,0:T(8,128)} %get-tuple-element.138, f32[8,10,10,768]{3,2,1,0:T(8,128)} %get-tuple-element.139, f32[8,10,10,768]{3,2,1,0:T(8,128)} %get-tuple-element.140, f32[8,10,10,768]{3,2,1,0:T(8,128)} %get-tuple-element.141, f32[8,10,10,768]{3,2,1,0:T(8,128)} %get-tuple-element.142, ...), kind=kLoop, calls=%fused_computation.66 | loop fusion | flops 66060288 | bytes 111968256 | tf_op jit(solution)/shard_map/transpose(jvp())/add_any | solution.py:29
  892.5 9.9 pad_add_fusion.1
  902.4 4.4 reshape.394
  906.8 0.9 pad_add_fusion.7
  907.8 3.5 multiply_add_fusion
  911.3 41.7 %all-reduce.99 = (f32[768]{0:T(1024)}, f32[768]{0:T(1024)}, f32[768]{0:T(1024)}, f32[768]{0:T(1024)}, f32[768]{0:T(1024)}) all-reduce(f32[768]{0:T(1024)S(1)} %get-tuple-element.62, f32[768]{0:T(1024)S(1)} %get-tuple-element.59, f32[768]{0:T(1024)S(1)} %get-tuple-element.61, ...), channel_id=1, replica_groups=mesh['dp'=8,'tensor'=4] {'dp','tensor'}, use_global_device_ids=true, to_apply=%region_57.58 | all-reduce | flops 3840 | bytes 30720 | tf_op jit(solution)/shard_map/psum | solution.py:119
  953.0 77.8 %all-reduce.104.cloned.1.call-done = f32[49,768]{1,0:T(8,128)} async-done(((f32[49,768]{1,0:T(8,128)}), f32[49,768]{1,0:T(8,128)}) %all-reduce.104.cloned.1.call-update) | async-done | bytes 150544 | tf_op jit(solution)/shard_map/psum | solution.py:119
  1030.8 1.7 copy.26
  1032.5 3.2 copy.27
  1035.7 1.4 copy.28
  (259 shorter events, 1.8 us)
Async XLA Ops:
  7.2 306.9 %copy-start = (bf16[768,768]{1,0:T(8,128)(2,1)S(1)}, bf16[768,768]{1,0:T(8,128)(2,1)}, u32[]{:S(2)}) copy-start(bf16[768,768]{1,0:T(8,128)(2,1)} %param.21) | copy-start | bytes 3538948
  7.2 213.6 %all-gather.3.cloned.1.call-start = ((), (), s32[]{:S(2)}) async-start(), calls=%async_computation.2 | async-start | bytes 6144000 | tf_op jit(solution)/shard_map/all_gather | solution.py:88
  8.9 13.2 %copy-start.8 = (f32[768]{0:T(1024)}, f32[768]{0:T(1024)S(1)}, u32[]{:S(2)}) copy-start(f32[768]{0:T(1024)S(1)} %get-tuple-element.103) | copy-start | bytes 9220
  8.9 13.2 %copy-start.10 = (f32[768]{0:T(1024)}, f32[768]{0:T(1024)S(1)}, u32[]{:S(2)}) copy-start(f32[768]{0:T(1024)S(1)} %get-tuple-element.104) | copy-start | bytes 9220
  8.9 13.2 %copy-start.12 = (f32[768]{0:T(1024)}, f32[768]{0:T(1024)S(1)}, u32[]{:S(2)}) copy-start(f32[768]{0:T(1024)S(1)} %get-tuple-element.105) | copy-start | bytes 9220
  8.9 13.2 %copy-start.14 = (f32[768]{0:T(1024)}, f32[768]{0:T(1024)S(1)}, u32[]{:S(2)}) copy-start(f32[768]{0:T(1024)S(1)} %get-tuple-element.106) | copy-start | bytes 9220
  8.9 13.2 %copy-start.16 = (f32[768]{0:T(1024)}, f32[768]{0:T(1024)S(1)}, u32[]{:S(2)}) copy-start(f32[768]{0:T(1024)S(1)} %get-tuple-element.107) | copy-start | bytes 9220
  8.9 13.2 %copy-start.18 = (f32[768]{0:T(1024)}, f32[768]{0:T(1024)S(1)}, u32[]{:S(2)}) copy-start(f32[768]{0:T(1024)S(1)} %get-tuple-element.108) | copy-start | bytes 9220
  9.0 13.2 %copy-start.20 = (f32[768]{0:T(1024)}, f32[768]{0:T(1024)S(1)}, u32[]{:S(2)}) copy-start(f32[768]{0:T(1024)S(1)} %get-tuple-element.109) | copy-start | bytes 9220
  9.0 13.2 %copy-start.80 = (f32[768]{0:T(1024)}, f32[768]{0:T(1024)S(1)}, u32[]{:S(2)}) copy-start(f32[768]{0:T(1024)S(1)} %get-tuple-element.102) | copy-start | bytes 9220
  9.0 13.2 %copy-start.82 = (f32[768]{0:T(1024)}, f32[768]{0:T(1024)S(1)}, u32[]{:S(2)}) copy-start(f32[768]{0:T(1024)S(1)} %get-tuple-element.110) | copy-start | bytes 9220
  9.7 12.6 %copy-start.32 = (f32[768]{0:T(1024)}, f32[768]{0:T(1024)S(1)}, u32[]{:S(2)}) copy-start(f32[768]{0:T(1024)S(1)} %get-tuple-element.97) | copy-start | bytes 9220
  9.7 12.6 %copy-start.34 = (f32[768]{0:T(1024)}, f32[768]{0:T(1024)S(1)}, u32[]{:S(2)}) copy-start(f32[768]{0:T(1024)S(1)} %get-tuple-element.98) | copy-start | bytes 9220
  9.7 12.6 %copy-start.36 = (f32[768]{0:T(1024)}, f32[768]{0:T(1024)S(1)}, u32[]{:S(2)}) copy-start(f32[768]{0:T(1024)S(1)} %get-tuple-element.99) | copy-start | bytes 9220
  9.7 12.6 %copy-start.38 = (f32[768]{0:T(1024)}, f32[768]{0:T(1024)S(1)}, u32[]{:S(2)}) copy-start(f32[768]{0:T(1024)S(1)} %get-tuple-element.100) | copy-start | bytes 9220
  9.7 12.6 %copy-start.40 = (f32[768]{0:T(1024)}, f32[768]{0:T(1024)S(1)}, u32[]{:S(2)}) copy-start(f32[768]{0:T(1024)S(1)} %get-tuple-element.101) | copy-start | bytes 9220
  9.7 12.6 %copy-start.44 = (f32[768]{0:T(1024)}, f32[768]{0:T(1024)S(1)}, u32[]{:S(2)}) copy-start(f32[768]{0:T(1024)S(1)} %get-tuple-element.84) | copy-start | bytes 9220
  121.8 99.0 %copy-start.89 = (bf16[768,768]{1,0:T(8,128)(2,1)S(1)}, bf16[768,768]{1,0:T(8,128)(2,1)}, u32[]{:S(2)}) copy-start(bf16[768,768]{1,0:T(8,128)(2,1)} %param.19) | copy-start | bytes 3538948
  125.3 188.8 %all-gather.5.cloned.1.call-start = ((), (), s32[]{:S(2)}) async-start(), calls=%async_computation.4 | async-start | bytes 6144000 | tf_op jit(solution)/shard_map/all_gather | solution.py:102
  126.1 391.7 %reduce-scatter.5.cloned.1.call-start = ((), (), s32[]{:S(2)}) async-start(), calls=%async_computation.5 | async-start | bytes 12288000 | tf_op jit(solution)/shard_map/reduce_scatter | solution.py:107
  351.7 336.9 %reduce-scatter.3.cloned.1.call-start = ((), (), s32[]{:S(2)}) async-start(), calls=%async_computation.3 | async-start | bytes 12288000 | tf_op jit(solution)/shard_map/reduce_scatter | solution.py:94
  371.8 25.4 %slice-start = ((s8[4915200]{0:T(1024)(128)(4,1)}), s8[720896]{0:T(1024)(128)(4,1)S(1)}, s32[]{:S(2)}) async-start(s8[4915200]{0:T(1024)(128)(4,1)} %bitcast.12), calls=%async_computation.8 | async-start | bytes 1441792
  371.8 581.2 %all-reduce.106.cloned.1.call-start = ((), (), s32[]{:S(2)}) async-start(), calls=%async_computation.7 | async-start | bytes 9437184 | tf_op jit(solution)/shard_map/psum | solution.py:116
  405.2 625.5 %all-reduce.104.cloned.1.call-start = ((), (), s32[]{:S(2)}) async-start(), calls=%async_computation.6 | async-start | bytes 344064 | tf_op jit(solution)/shard_map/psum | solution.py:119
  521.3 167.3 %copy-start.3 = (bf16[800,768]{1,0:T(8,128)(2,1)S(1)}, bf16[800,768]{1,0:T(8,128)(2,1)}, u32[]{:S(2)}) copy-start(bf16[800,768]{1,0:T(8,128)(2,1)} %param.14) | copy-start | bytes 3686404
  521.3 167.3 %copy-start.7 = (f32[800]{0:T(1024)S(1)}, f32[800]{0:T(1024)}, u32[]{:S(2)}) copy-start(f32[800]{0:T(1024)} %copy-done.6) | copy-start | bytes 9604
  729.3 26.3 %copy-start.81 = (f32[768]{0:T(1024)S(1)}, f32[768]{0:T(1024)}, u32[]{:S(2)}) copy-start(f32[768]{0:T(1024)} %copy-done.80) | copy-start | bytes 9220
  729.3 26.3 %copy-start.83 = (f32[768]{0:T(1024)S(1)}, f32[768]{0:T(1024)}, u32[]{:S(2)}) copy-start(f32[768]{0:T(1024)} %copy-done.82) | copy-start | bytes 9220
  755.6 24.7 %copy-start.2 = (f32[8,10,10,768]{3,2,1,0:T(8,128)S(1)}, f32[8,10,10,768]{3,2,1,0:T(8,128)}, u32[]{:S(2)}) copy-start(f32[8,10,10,768]{3,2,1,0:T(8,128)} %reshape.393) | copy-start | bytes 7372804
  790.8 23.0 %copy-start.9 = (f32[768]{0:T(1024)S(1)}, f32[768]{0:T(1024)}, u32[]{:S(2)}) copy-start(f32[768]{0:T(1024)} %copy-done.8) | copy-start | bytes 9220
  790.8 23.0 %copy-start.11 = (f32[768]{0:T(1024)S(1)}, f32[768]{0:T(1024)}, u32[]{:S(2)}) copy-start(f32[768]{0:T(1024)} %copy-done.10) | copy-start | bytes 9220
  790.8 23.0 %copy-start.13 = (f32[768]{0:T(1024)S(1)}, f32[768]{0:T(1024)}, u32[]{:S(2)}) copy-start(f32[768]{0:T(1024)} %copy-done.12) | copy-start | bytes 9220
  790.8 23.0 %copy-start.15 = (f32[768]{0:T(1024)S(1)}, f32[768]{0:T(1024)}, u32[]{:S(2)}) copy-start(f32[768]{0:T(1024)} %copy-done.14) | copy-start | bytes 9220
  790.8 23.0 %copy-start.17 = (f32[768]{0:T(1024)S(1)}, f32[768]{0:T(1024)}, u32[]{:S(2)}) copy-start(f32[768]{0:T(1024)} %copy-done.16) | copy-start | bytes 9220
  790.9 23.0 %copy-start.19 = (f32[768]{0:T(1024)S(1)}, f32[768]{0:T(1024)}, u32[]{:S(2)}) copy-start(f32[768]{0:T(1024)} %copy-done.18) | copy-start | bytes 9220
  790.9 23.0 %copy-start.21 = (f32[768]{0:T(1024)S(1)}, f32[768]{0:T(1024)}, u32[]{:S(2)}) copy-start(f32[768]{0:T(1024)} %copy-done.20) | copy-start | bytes 9220
  790.9 23.0 %copy-start.23 = (f32[768]{0:T(1024)S(1)}, f32[768]{0:T(1024)}, u32[]{:S(2)}) copy-start(f32[768]{0:T(1024)} %copy-done.22) | copy-start | bytes 9220
  790.9 23.0 %copy-start.25 = (f32[768]{0:T(1024)S(1)}, f32[768]{0:T(1024)}, u32[]{:S(2)}) copy-start(f32[768]{0:T(1024)} %copy-done.24) | copy-start | bytes 9220
  790.9 23.0 %copy-start.27 = (f32[768]{0:T(1024)S(1)}, f32[768]{0:T(1024)}, u32[]{:S(2)}) copy-start(f32[768]{0:T(1024)} %copy-done.26) | copy-start | bytes 9220
  790.9 23.0 %copy-start.29 = (f32[768]{0:T(1024)S(1)}, f32[768]{0:T(1024)}, u32[]{:S(2)}) copy-start(f32[768]{0:T(1024)} %copy-done.28) | copy-start | bytes 9220
  790.9 23.0 %copy-start.31 = (f32[768]{0:T(1024)S(1)}, f32[768]{0:T(1024)}, u32[]{:S(2)}) copy-start(f32[768]{0:T(1024)} %copy-done.30) | copy-start | bytes 9220
  790.9 23.0 %copy-start.33 = (f32[768]{0:T(1024)S(1)}, f32[768]{0:T(1024)}, u32[]{:S(2)}) copy-start(f32[768]{0:T(1024)} %copy-done.32) | copy-start | bytes 9220
  790.9 23.0 %copy-start.35 = (f32[768]{0:T(1024)S(1)}, f32[768]{0:T(1024)}, u32[]{:S(2)}) copy-start(f32[768]{0:T(1024)} %copy-done.34) | copy-start | bytes 9220
  790.9 23.0 %copy-start.37 = (f32[768]{0:T(1024)S(1)}, f32[768]{0:T(1024)}, u32[]{:S(2)}) copy-start(f32[768]{0:T(1024)} %copy-done.36) | copy-start | bytes 9220
  791.0 23.0 %copy-start.39 = (f32[768]{0:T(1024)S(1)}, f32[768]{0:T(1024)}, u32[]{:S(2)}) copy-start(f32[768]{0:T(1024)} %copy-done.38) | copy-start | bytes 9220
  791.0 23.0 %copy-start.41 = (f32[768]{0:T(1024)S(1)}, f32[768]{0:T(1024)}, u32[]{:S(2)}) copy-start(f32[768]{0:T(1024)} %copy-done.40) | copy-start | bytes 9220
  791.0 23.0 %copy-start.43 = (f32[768]{0:T(1024)S(1)}, f32[768]{0:T(1024)}, u32[]{:S(2)}) copy-start(f32[768]{0:T(1024)} %copy-done.42) | copy-start | bytes 9220
  953.0 82.7 %copy-start.5 = (f32[768,768]{1,0:T(8,128)S(1)}, f32[768,768]{1,0:T(8,128)}, u32[]{:S(2)}) copy-start(f32[768,768]{1,0:T(8,128)} %get-tuple-element.192) | copy-start | bytes 7077892
  (51 other events, 519.8 us)
Sparse Core Ops, SparseCore 0:
  125.4 95.3 all-gather.2
  223.0 91.0 all-gather.4
  351.8 165.9 reduce-scatter.4
  520.1 168.4 reduce-scatter.2
  693.0 87.9 all-reduce.105
  907.9 122.8 all-reduce.103
where the time goes:
time: 1050 us; the launch traced here: 1040 us
  waiting for transfers between devices  533 us (51%)
  other arithmetic  338 us (32%)
  matrix products  70.9 us (7%)
  blocking collectives  56.6 us (5%)
  local copies, waits for them, and re-layouts  29.2 us (3%)
  between operations  16.2 us (2%)
    reduce_scatter x1, waiting for transfers between devices, per_device(): lax.psum_scatter(jnp.dot(active, reduce_weight, preferred_element_type=jn...  163 us
    reduce_scatter x1, waiting for transfers between devices, per_device(): lax.psum_scatter(contract_cols(hidden_cot, expand_weight), 'tensor', scat...  113 us
    all_gather x1, waiting for transfers between devices, per_device(): lax.all_gather(normed, 'tensor', axis=0, tiled=True)  94.2 us
    reduce_sum x1, other arithmetic, front_part(): center = jnp.mean(mixed, axis=1, keepdims=True)  91.9 us
    all_gather x1, waiting for transfers between devices, per_device(): cot_group = lax.all_gather(branch_cot, 'tensor', axis=0, tiled=True)  84.4 us
    reduce_sum x3, other arithmetic, front_part(): mixed = mixed + window * kernel[offset_row * KERNEL + offset_col]  82.4 us
    psum x1, waiting for transfers between devices, per_device(): lax.psum((kernel_grad, depth_bias_grad, gain_grad, shift_grad, reduce_bia...  77.8 us
    add_any x2, other arithmetic, front_part(): padded[:, offset_row:offset_row + SIDE, offset_col:offset_col + SIDE, :]  65.4 us
  transfers between devices with their start and end apart: 6, of which 5 were waited for; matrix products, arithmetic and copies ran while one was open for 26% of the time, Pallas kernels for 0%

commit v1 on v0

v1 whole, which is shorter than its diff:
```python
import functools
import math
import jax
import jax.numpy as jnp
from jax import lax
from jax.experimental import pallas as pl
from jax.experimental.pallas import tpu as pltpu
from jax.sharding import PartitionSpec as P

KERNEL = 7
SIDE = 10
PLACES = SIDE * SIDE
TAPS = KERNEL * KERNEL
MARGIN = KERNEL // 2
LANES = 128
BLOCK = 256
norm_eps = 1e-06
f32 = jnp.float32
bf16 = jnp.bfloat16
MESH = pl.DeviceIdType.MESH
ROW_BIAS, ROW_GAIN, ROW_SHIFT, ROW_REDUCE, ROW_SCALE, ROW_EXPAND = 49, 50, 51, 52, 53, 54
SMALL = 64


def gelu_both(h):
    a = jnp.abs(h)
    t = 1.0 / (1.0 + a * (0.3275911 / math.sqrt(2.0)))
    e = jnp.exp(h * h * -0.5)
    poly = t * (
        0.254829592
        + t * (-0.284496736 + t * (1.421413741 + t * (-1.453152027 + t * 1.061405429)))
    )
    q = 0.5 * e * poly
    phi = jnp.where(h >= 0.0, 1.0 - q, q)
    return h * phi, phi + h * (e * (1.0 / math.sqrt(2.0 * math.pi)))


def dot(a, b):
    return jnp.dot(a, b, preferred_element_type=f32)


def dot_t(a, b):
    return lax.dot_general(a, b, (((1,), (1,)), ((), ())), preferred_element_type=f32)


def kernel(
    n_dp,
    n_tensor,
    pix_hbm,
    side_ref,
    cot_hbm,
    taps_ref,
    depth_bias_ref,
    gain_ref,
    shift_ref,
    we_hbm,
    eb_ref,
    wr_hbm,
    rb_ref,
    scale_ref,
    out_hbm,
    in_grad_hbm,
    gr_hbm,
    ge_hbm,
    small_hbm,
    stage,
    X,
    XH,
    RSTD,
    NM,
    CM,
    BC,
    KB,
    NT,
    BT,
    WE,
    WR,
    EB,
    ACT,
    HC,
    EBG,
    NC,
    KG,
    ACC,
    GS,
    R0,
    R1,
    R2,
    RZ,
    RX,
    OUTB,
    S,
    SR,
    SZ,
    SX,
    SALL,
    load_sem,
    out_sem,
    w_send,
    w_recv,
    e_send,
    e_recv,
    g_send,
    g_recv,
    x_send,
    x_recv,
    s_send,
    s_recv,
):
    D = NM.shape[1]
    G = D // LANES
    ROWS = NM.shape[0]
    IMG = ROWS // PLACES
    HALF, QUART, PIECE = D // 2, D // 4, D // 8
    SLOTS = n_tensor
    extra = n_dp.bit_length() - 4
    dp = lax.axis_index("dp")
    tz = lax.axis_index("tensor")
    core = lax.rem(dp, 2)
    xb = lax.rem(lax.div(dp, 2), 2)
    yb = lax.rem(lax.div(dp, 4), 2)
    low = lax.rem(dp, 8)
    bits = (core, xb, yb)

    def flip(b):
        bit = bits[b] if b < 3 else lax.rem(lax.div(dp, 1 << b), 2)
        return dp + (1 - 2 * bit) * (1 << b)

    def flip_low(j):
        d = dp
        for b in range(3):
            if j >> b & 1:
                d = d + (1 - 2 * bits[b]) * (1 << b)
        return d

    OFF = [0, 1, n_tensor - 1] + list(range(2, n_tensor - 1))

    peers = [(flip_low(j), tz) for j in range(1, 8)]
    peers += [(dp, lax.rem(tz + o, n_tensor)) for o in range(1, n_tensor)]
    peers += [(flip(b), tz) for b in range(3, 3 + extra)]
    barrier = pltpu.get_barrier_semaphore()
    for peer in peers:
        pl.semaphore_signal(barrier, inc=1, device_id=peer, device_id_type=MESH)

    loads = [
        pltpu.make_async_copy(pix_hbm, NM, load_sem.at[0]),
        pltpu.make_async_copy(cot_hbm, BC, load_sem.at[1]),
        pltpu.make_async_copy(we_hbm, WE.at[0], load_sem.at[2]),
        pltpu.make_async_copy(wr_hbm, WR.at[0], load_sem.at[3]),
    ]
    for copy in loads:
        copy.start()

    def remote(src, dst, send, recv, device):
        return pltpu.make_async_remote_copy(
            src_ref=src, dst_ref=dst, send_sem=send, recv_sem=recv,
            device_id=device, device_id_type=MESH,
        )

    W = (WE, WR)
    first = (xb, yb)
    second = (yb, xb)
    first_peer = (flip(1), flip(2))
    second_peer = (flip(2), flip(1))

    def w_rows(m, level):
        start = core * HALF
        if level <= 2:
            start = start + second[m] * QUART
        if level <= 1:
            start = start + first[m] * PIECE
        size = (PIECE, PIECE, QUART, HALF)[level]
        return pl.ds(pl.multiple_of(start, 16), size)

    def w_copy(s, m, level):
        rows = w_rows(m, level)
        here = W[m].at[s, rows, :]
        src = here
        if level == 0:
            src = (we_hbm, wr_hbm)[m].at[rows, :]
            device = (dp, lax.rem(tz + n_tensor - OFF[s], n_tensor))
        elif level == 1:
            device = (first_peer[m], tz)
        elif level == 2:
            device = (second_peer[m], tz)
        else:
            device = (flip(0), tz)
        return remote(src, here, w_send.at[s - 1, m, level], w_recv.at[s - 1, m, level], device)

    def e_copy(s):
        device = (dp, lax.rem(tz + n_tensor - OFF[s], n_tensor))
        return remote(EB.at[0], EB.at[s], e_send.at[s - 1], e_recv.at[s - 1], device)

    def w_step(s, level):
        for m in range(2):
            if level > 0:
                w_copy(s, m, level - 1).wait_recv()
            if level < 4:
                w_copy(s, m, level).start()
        if level == 4:
            e_copy(s).wait_recv()

    EB[0] = jnp.broadcast_to(eb_ref[...].astype(f32), (8, D))
    pl.semaphore_wait(barrier, len(peers))
    for s in range(1, SLOTS):
        w_step(s, 0)
        e_copy(s).start()

    g_first = (yb, xb)
    g_second = (xb, yb)
    g_first_peer = (flip(2), flip(1))
    g_second_peer = (flip(1), flip(2))

    def g_start(m, level):
        start = core * HALF
        if level >= 1:
            start = start + g_first[m] * QUART
        if level >= 2:
            start = start + g_second[m] * PIECE
        return start

    def g_copy(s, m, level):
        if level == 0:
            start, size, peer, dst = (1 - core) * HALF, HALF, flip(0), R0
        elif level == 1:
            start = g_start(m, 0) + (1 - g_first[m]) * QUART
            size, peer, dst = QUART, g_first_peer[m], R1
        else:
            start = g_start(m, 1) + (1 - g_second[m]) * PIECE
            size, peer, dst = PIECE, g_second_peer[m], R2
        src = GS.at[s, m, pl.ds(pl.multiple_of(start, 16), size), :]
        return remote(
            src, dst.at[s, m], g_send.at[s, m, level], g_recv.at[s, m, level], (peer, tz)
        )

    def z_copy(s, m):
        src = GS.at[s, m, pl.ds(pl.multiple_of(g_start(m, 2), 16), PIECE), :]
        device = (dp, lax.rem(tz + OFF[s], n_tensor))
        return remote(src, RZ.at[s - 1, m], g_send.at[s, m, 3], g_recv.at[s, m, 3], device)

    def g_step(s, level):
        for m in range(2):
            if level > 0:
                g_copy(s, m, level - 1).wait_recv()
                got = (R0, R1, R2)[level - 1]
                start = g_start(m, level - 1)
                size = (HALF, QUART, PIECE)[level - 1]

                def add(i, c):
                    rows = pl.ds(pl.multiple_of(start + i * 16, 16), 16)
                    GS[s, m, rows, :] = (
                        GS[s, m, rows, :] + got[s, m, pl.ds(pl.multiple_of(i * 16, 16), 16), :]
                    )
                    return c

                lax.fori_loop(0, size // 16, add, 0)
            if level < 3:
                g_copy(s, m, level).start()
            elif s > 0:
                z_copy(s, m).start()

    def a_copy(m, level):
        if level == 0:
            start, size, peer = g_start(m, 2), PIECE, g_second_peer[m]
        elif level == 1:
            start, size, peer = g_start(m, 1), QUART, g_first_peer[m]
        else:
            start, size, peer = g_start(m, 0), HALF, flip(0)
        here = OUTB.at[m, pl.ds(pl.multiple_of(start, 16), size), :]
        return remote(here, here, g_send.at[0, m, 3 + level], g_recv.at[0, m, 3 + level], (peer, tz))

    def x_copy(m, b):
        here = OUTB.at[m, pl.ds(pl.multiple_of(g_start(m, 2), 16), PIECE), :]
        return remote(here, RX.at[b - 3, m], x_send.at[b - 3, m], x_recv.at[b - 3, m], (flip(b), tz))

    def finish_sum():
        for m in range(2):
            for s in range(1, SLOTS):
                z_copy(s, m).wait_recv()
            start = g_start(m, 2)

            def add(i, c):
                rows = pl.ds(pl.multiple_of(start + i * 16, 16), 16)
                own = pl.ds(pl.multiple_of(i * 16, 16), 16)
                total = GS[0, m, rows, :].astype(f32)
                for s in range(1, SLOTS):
                    total = total + RZ[s - 1, m, own, :].astype(f32)
                OUTB[m, rows, :] = total.astype(bf16)
                return c

            lax.fori_loop(0, PIECE // 16, add, 0)
            for b in range(3, 3 + extra):
                x_copy(m, b).start()
                x_copy(m, b).wait()

                def add_x(i, c):
                    rows = pl.ds(pl.multiple_of(start + i * 16, 16), 16)
                    OUTB[m, rows, :] = (
                        OUTB[m, rows, :] + RX[b - 3, m, pl.ds(pl.multiple_of(i * 16, 16), 16), :]
                    )
                    return c

                lax.fori_loop(0, PIECE // 16, add_x, 0)
            a_copy(m, 0).start()

    def a_step(level):
        for m in range(2):
            a_copy(m, level - 1).wait_recv()
            if level < 3:
                a_copy(m, level).start()

    def sr_copy(j):
        dst_low = flip_low(j)
        rows = pl.ds(pl.multiple_of(lax.rem(dst_low, 8) * 8, 8), 8)
        return remote(S.at[rows, :], SR.at[j - 1], s_send.at[0, j], s_recv.at[0, j], (dst_low, tz))

    def sz_copy(o):
        return remote(
            SZ.at[tz], SZ.at[tz], s_send.at[1, o], s_recv.at[1, o],
            (dp, lax.rem(tz + o, n_tensor)),
        )

    own_small = pl.ds(pl.multiple_of(low * 8, 8), 8)

    def sa_copy(j):
        here = SALL.at[own_small, :]
        return remote(here, here, s_send.at[2, j], s_recv.at[2, j], (flip_low(j), tz))

    def sx_copy(b):
        return remote(
            SALL.at[own_small, :], SX.at[b - 3], s_send.at[3, b], s_recv.at[3, b], (flip(b), tz)
        )

    def small_step(level):
        if level == 0:
            for j in range(1, 8):
                sr_copy(j).start()
        elif level == 1:
            total = S[own_small, :]
            for j in range(1, 8):
                sr_copy(j).wait_recv()
                total = total + SR[j - 1]
            SZ[tz] = total
            for o in range(1, n_tensor):
                sz_copy(o).start()
        elif level == 2:
            for o in range(1, n_tensor):
                sz_copy(o).wait_recv()
            total = SZ[0]
            for o in range(1, n_tensor):
                total = total + SZ[o]
            SALL[own_small, :] = total
            for b in range(3, 3 + extra):
                sx_copy(b).start()
                sx_copy(b).wait()
                SALL[own_small, :] = SALL[own_small, :] + SX[b - 3]
            for j in range(1, 8):
                sa_copy(j).start()
        else:
            for j in range(1, 8):
                sa_copy(j).wait_recv()

    row = lax.broadcasted_iota(jnp.int32, (IMG, LANES), 0)
    sides = jnp.zeros((IMG, LANES), jnp.int32)
    for i in range(IMG):
        sides = jnp.where(row == i, side_ref[i], sides)

    def mask_at(p):
        if isinstance(p, int):
            return jnp.where(sides > max(p // SIDE, p % SIDE), 1.0, 0.0)
        return jnp.where(sides > jnp.maximum(lax.div(p, SIDE), lax.rem(p, SIDE)), 1.0, 0.0)

    def lanes(g):
        return slice(g * LANES, (g + 1) * LANES)

    def place(p):
        return pl.ds(p * IMG, IMG)

    def spread(src):
        def body(i, c):
            rows = pl.ds(pl.multiple_of(i * 80, 16), 80)
            for g in range(G):
                stage[g, rows, :] = src[rows, lanes(g)].astype(f32)
            return c

        lax.fori_loop(0, ROWS // 80, body, 0)

    def load_pixels():
        def body(p, c):
            m = mask_at(p)
            rows = pl.ds(pl.multiple_of(p * IMG, IMG), IMG)
            for g in range(G):
                X[g, rows, :] = stage[g, pl.ds(p, IMG, stride=PLACES), :] * m
            return c

        lax.fori_loop(0, PLACES, body, 0, unroll=2)

    def load_cot():
        scale = scale_ref[...].astype(f32)

        def body(q, sums):
            sums = list(sums)
            masks = [mask_at(2 * q + u) for u in range(2)]
            rows = pl.ds(pl.multiple_of(q * 2 * IMG, 2 * IMG), 2 * IMG)
            for g in range(G):
                c = [stage[g, pl.ds(2 * q + u, IMG, stride=PLACES), :] * masks[u] for u in range(2)]
                c = jnp.concatenate(c, axis=0)
                CM[rows, lanes(g)] = c.astype(bf16)
                b = (c * scale[:, lanes(g)]).astype(bf16)
                BC[rows, lanes(g)] = b
                b = b.astype(f32)
                sums[g] = sums[g] + (b[:IMG] + b[IMG:])
            return tuple(sums)

        zero = jnp.zeros((IMG, LANES), f32)
        sums = lax.fori_loop(0, PLACES // 2, body, (zero,) * G)
        for g in range(G):
            ACC[3, g] = sums[g]

    def load_taps():
        for g in range(G):
            for t in range(TAPS):
                KB[g, place(t), :] = jnp.broadcast_to(
                    taps_ref[t : t + 1, lanes(g)].astype(f32), (IMG, LANES)
                )

    def conv(src, dst, bias, flipped, post, between):
        def one(g, carry):
            for r in range(SIDE):
                acc = [None] * SIDE if bias is None else [bias[g]] * SIDE
                for rr in range(max(0, r - MARGIN), min(SIDE, r + MARGIN + 1)):
                    xs = [src[g, place(rr * SIDE + c), :] for c in range(SIDE)]
                    for dc in range(KERNEL):
                        t = (rr - r + MARGIN) * KERNEL + dc
                        k = KB[g, place(TAPS - 1 - t if flipped else t), :]
                        for c in range(SIDE):
                            cc = c + dc - MARGIN
                            if 0 <= cc < SIDE:
                                v = xs[cc] * k
                                acc[c] = v if acc[c] is None else acc[c] + v
                if post is None:
                    for c in range(SIDE):
                        dst[g, place(r * SIDE + c), :] = acc[c]
                else:
                    post(g, r, acc)
            between(g)
            return carry

        lax.fori_loop(0, G, one, 0)

    def layernorm():
        gain = gain_ref[...].astype(f32)
        shift = shift_ref[...].astype(f32)

        def body(q, c):
            rows = pl.ds(pl.multiple_of(q * 16, 16), 16)
            v = [XH[g, rows, :] for g in range(G)]
            total = functools.reduce(jnp.add, v)
            mean = jnp.sum(total, axis=1, keepdims=True) * (1.0 / D)
            v = [a - mean for a in v]
            total = functools.reduce(jnp.add, [a * a for a in v])
            rstd = lax.rsqrt(jnp.sum(total, axis=1, keepdims=True) * (1.0 / D) + norm_eps)
            RSTD[rows, :] = jnp.broadcast_to(rstd, (16, LANES))
            for g in range(G):
                xh = v[g] * rstd
                XH[g, rows, :] = xh
                NM[rows, lanes(g)] = (xh * gain[:, lanes(g)] + shift[:, lanes(g)]).astype(bf16)
            return c

        lax.fori_loop(0, ROWS // 16, body, 0, unroll=2)

    def layernorm_back():
        gain = gain_ref[...].astype(f32)

        def body(q, sums):
            gains, shifts, biases = [list(part) for part in sums]
            rows = pl.ds(pl.multiple_of(q * 16, 16), 16)
            rstd = RSTD[rows, :]
            xh = [XH[g, rows, :] for g in range(G)]
            nc = [NC[g, rows, :] for g in range(G)]
            d = [nc[g] * gain[:, lanes(g)] for g in range(G)]
            s1 = functools.reduce(jnp.add, d)
            s2 = functools.reduce(jnp.add, [d[g] * xh[g] for g in range(G)])
            m1 = jnp.sum(s1, axis=1, keepdims=True) * (1.0 / D)
            m2 = jnp.sum(s2, axis=1, keepdims=True) * (1.0 / D)
            for g in range(G):
                dm = rstd * (d[g] - m1 - xh[g] * m2)
                NC[g, rows, :] = dm
                gx = nc[g] * xh[g]
                gains[g] = gains[g] + (gx[:8] + gx[8:])
                shifts[g] = shifts[g] + (nc[g][:8] + nc[g][8:])
                biases[g] = biases[g] + (dm[:8] + dm[8:])
            return tuple(gains), tuple(shifts), tuple(biases)

        zeros = (jnp.zeros((8, LANES), f32),) * G
        sums = lax.fori_loop(0, ROWS // 16, body, (zeros, zeros, zeros))
        for i in range(3):
            for g in range(G):
                ACC[i, g] = sums[i][g]

    def kernel_grad():
        def one(g, carry):
            for dr in range(KERNEL):
                acc = [[None, None] for _ in range(KERNEL)]
                for r in range(SIDE):
                    rr = r + dr - MARGIN
                    if not 0 <= rr < SIDE:
                        continue
                    ds = [NC[g, place(r * SIDE + c), :] for c in range(SIDE)]
                    xs = [X[g, place(rr * SIDE + c), :] for c in range(SIDE)]
                    for dc in range(KERNEL):
                        a = acc[dc]
                        for c in range(SIDE):
                            cc = c + dc - MARGIN
                            if 0 <= cc < SIDE:
                                v = ds[c] * xs[cc]
                                a[c % 2] = v if a[c % 2] is None else a[c % 2] + v
                for dc in range(KERNEL):
                    KG[g, place(dr * KERNEL + dc), :] = acc[dc][0] + acc[dc][1]
            return carry

        lax.fori_loop(0, G, one, 0)

    def hidden_block(s, j):
        cols = slice(j * BLOCK, (j + 1) * BLOCK)
        h = dot(NM[...], WE[s, :, cols])
        stage[0] = h[:, :LANES]
        stage[1] = h[:, LANES:]
        a = dot_t(BC[...], WR[s, cols, :])
        stage[2] = a[:, :LANES]
        stage[3] = a[:, LANES:]

        def body(i, sums):
            rows = pl.ds(pl.multiple_of(i * 16, 16), 16)
            out = []
            for u in range(2):
                mine = slice(j * BLOCK + u * LANES, j * BLOCK + (u + 1) * LANES)
                value, slope = gelu_both(stage[u, rows, :] + EB[s, 0:1, mine])
                ACT[s, rows, mine] = value.astype(bf16)
                w = (stage[2 + u, rows, :] * slope).astype(bf16)
                HC[s, rows, mine] = w
                w = w.astype(f32)
                out.append(sums[u] + (w[:8] + w[8:]))
            return tuple(out)

        zero = jnp.zeros((8, LANES), f32)
        sums = lax.fori_loop(0, ROWS // 16, body, (zero, zero), unroll=5)
        for u in range(2):
            EBG[s, :, j * BLOCK + u * LANES : j * BLOCK + (u + 1) * LANES] = sums[u]

    def grad_block(s, j):
        cols = slice(j * BLOCK, (j + 1) * BLOCK)
        GS[s, 0, :, cols] = dot(BT[...], ACT[s, :, cols]).astype(bf16)
        GS[s, 1, :, cols] = dot(NT[...], HC[s, :, cols]).astype(bf16)

    def back_to_normed():
        for n in range(D // BLOCK):
            cols = slice(n * BLOCK, (n + 1) * BLOCK)
            total = dot_t(HC[0], WE[0, cols, :])
            for s in range(1, SLOTS):
                total = total + dot_t(HC[s], WE[s, cols, :])
            NC[2 * n] = total[:, :LANES]
            NC[2 * n + 1] = total[:, LANES:]

    def to_branch():
        for n in range(D // BLOCK):
            cols = slice(n * BLOCK, (n + 1) * BLOCK)
            total = dot(ACT[0], WR[0, :, cols])
            for s in range(1, SLOTS):
                total = total + dot(ACT[s], WR[s, :, cols])
            XH[2 * n] = total[:, :LANES]
            XH[2 * n + 1] = total[:, LANES:]

    def block_output():
        scale = scale_ref[...].astype(f32)
        shift = rb_ref[...].astype(f32)

        def body(q, sums):
            sums = list(sums)
            rows = pl.ds(pl.multiple_of(q * 2 * IMG, 2 * IMG), 2 * IMG)
            masks = jnp.concatenate([mask_at(2 * q + u) for u in range(2)], axis=0)
            for g in range(G):
                branch = XH[g, rows, :] + shift[:, lanes(g)]
                v = CM[rows, lanes(g)].astype(f32) * branch
                sums[g] = sums[g] + (v[:IMG] + v[IMG:])
                value = X[g, rows, :] + masks * (scale[:, lanes(g)] * branch)
                for u in range(2):
                    stage[g, pl.ds(2 * q + u, IMG, stride=PLACES), :] = value[u * IMG : (u + 1) * IMG]
            return tuple(sums)

        zero = jnp.zeros((IMG, LANES), f32)
        sums = lax.fori_loop(0, PLACES // 2, body, (zero,) * G)
        for g in range(G):
            ACC[4, g] = sums[g]

        def narrow(i, c):
            rows = pl.ds(pl.multiple_of(i * 80, 16), 80)
            for g in range(G):
                NM[rows, lanes(g)] = stage[g, rows, :].astype(bf16)
            return c

        lax.fori_loop(0, ROWS // 80, narrow, 0)

    def small_sums():
        S[...] = jnp.zeros_like(S)
        for g in range(G):
            for t in range(TAPS):
                S[t : t + 1, lanes(g)] = jnp.sum(KG[g, place(t), :], axis=0, keepdims=True)
            for r, i in ((ROW_BIAS, 2), (ROW_GAIN, 0), (ROW_SHIFT, 1), (ROW_REDUCE, 3), (ROW_SCALE, 4)):
                S[r : r + 1, lanes(g)] = jnp.sum(ACC[i, g], axis=0, keepdims=True)
        for s in range(SLOTS):
            r = ROW_EXPAND + lax.rem(tz + OFF[s], n_tensor)
            S[pl.ds(r, 1), :] = jnp.sum(EBG[s], axis=0, keepdims=True)

    loads[0].wait()
    spread(NM)
    load_pixels()
    load_taps()
    w_plan = [[(1, 1)], [(2, 1), (1, 2)], [(1, 3)], [(2, 2)], [(3, 1)], [(2, 3), (1, 4)]]

    def during_conv(g):
        for i in range(G):
            @pl.when(g == i)
            def _():
                for s, level in w_plan[i] if i < len(w_plan) else []:
                    w_step(s, level)

    biases = depth_bias_ref[...].astype(f32)
    for g in range(G):
        ACC[0, g] = jnp.broadcast_to(biases[:, lanes(g)], (8, LANES))
    conv(X, XH, ACC.at[0], False, None, during_conv)
    loads[1].wait()
    spread(BC)
    load_cot()
    layernorm()
    w_step(3, 2)
    NT[...] = NM[...].T
    BT[...] = BC[...].T
    loads[2].wait()
    loads[3].wait()
    for s in range(SLOTS):
        if s == 2:
            w_step(2, 4)
        if s == 3:
            w_step(3, 4)
        for j in range(D // BLOCK):
            hidden_block(s, j)
            if s == 0 and j == 0:
                w_step(3, 3)
            if s > 0 and j == 0:
                g_step(s - 1, 1)
            if s > 1 and j == 1:
                g_step(s - 2, 3)
        for j in range(D // BLOCK):
            grad_block(s, j)
        g_step(s, 0)
        if s > 0:
            g_step(s - 1, 2)
    last = SLOTS - 1
    back_to_normed()
    g_step(last, 1)
    g_step(last - 1, 3)
    layernorm_back()
    g_step(last, 2)
    kernel_grad()
    g_step(last, 3)
    to_branch()
    finish_sum()
    block_output()
    pltpu.make_async_copy(NM, out_hbm, out_sem.at[0]).start()
    small_sums()
    small_step(0)
    a_step(1)
    small_step(1)

    def finish_input(g, r, acc):
        cols = pl.ds(pl.multiple_of(g * LANES, LANES), LANES)
        for c in range(0, SIDE, 2):
            p = r * SIDE + c
            cot = CM[pl.ds(p * IMG, 2 * IMG), cols].astype(f32)
            for u in range(2):
                XH[g, pl.ds(p + u, IMG, stride=PLACES), :] = (
                    acc[c + u] * mask_at(p + u) + cot[u * IMG : (u + 1) * IMG]
                )

    def out_copy(g):
        return pltpu.make_async_copy(
            XH.at[g], in_grad_hbm.at[:, pl.ds(pl.multiple_of(g * LANES, LANES), LANES)], out_sem.at[1 + g]
        )

    def during_back(g):
        out_copy(g).start()

        @pl.when(g == 1)
        def _():
            a_step(2)
            small_step(2)

        @pl.when(g == 4)
        def _():
            a_step(3)

    conv(NC, None, None, True, finish_input, during_back)
    small_step(3)
    tail = [
        pltpu.make_async_copy(OUTB.at[0], gr_hbm, load_sem.at[0]),
        pltpu.make_async_copy(OUTB.at[1], ge_hbm, load_sem.at[1]),
        pltpu.make_async_copy(SALL, small_hbm, load_sem.at[2]),
    ]
    for copy in tail:
        copy.start()
    for s in range(1, SLOTS):
        e_copy(s).wait_send()
        for m in range(2):
            for level in range(4):
                w_copy(s, m, level).wait_send()
            z_copy(s, m).wait_send()
    for s in range(SLOTS):
        for m in range(2):
            for level in range(3):
                g_copy(s, m, level).wait_send()
    for m in range(2):
        for level in range(3):
            a_copy(m, level).wait_send()
    for j in range(1, 8):
        sr_copy(j).wait_send()
        sa_copy(j).wait_send()
    for o in range(1, n_tensor):
        sz_copy(o).wait_send()
    pltpu.make_async_copy(NM, out_hbm, out_sem.at[0]).wait()
    for g in range(G):
        out_copy(g).wait()
    for copy in tail:
        copy.wait()


def per_device(
    n_dp,
    n_tensor,
    pixels,
    crop_sides,
    out_cotangent,
    depth_kernel,
    depth_bias,
    norm_gain,
    norm_shift,
    expand_weight,
    expand_bias,
    reduce_weight,
    reduce_bias,
    layer_scale,
):
    rows, D = pixels.shape
    G = D // LANES
    img = rows // PLACES
    slots = n_tensor
    extra = max(n_dp.bit_length() - 4, 1)
    vmem = pl.BlockSpec(memory_space=pltpu.VMEM)
    hbm = pl.BlockSpec(memory_space=pl.ANY)
    smem = pl.BlockSpec(memory_space=pltpu.SMEM)
    V = pltpu.VMEM
    DMA = pltpu.SemaphoreType.DMA
    scratch = [
        V((G, rows, LANES), f32),
        V((G, rows, LANES), f32),
        V((G, rows, LANES), f32),
        V((rows, LANES), f32),
        V((rows, D), bf16),
        V((rows, D), bf16),
        V((rows, D), bf16),
        V((G, TAPS * img, LANES), f32),
        V((D, rows), bf16),
        V((D, rows), bf16),
        V((slots, D, D), bf16),
        V((slots, D, D), bf16),
        V((slots, 8, D), f32),
        V((slots, rows, D), bf16),
        V((slots, rows, D), bf16),
        V((slots, 8, D), f32),
        V((G, rows, LANES), f32),
        V((G, TAPS * img, LANES), f32),
        V((5, G, 8, LANES), f32),
        V((slots, 2, D, D), bf16),
        V((slots, 2, D // 2, D), bf16),
        V((slots, 2, D // 4, D), bf16),
        V((slots, 2, D // 8, D), bf16),
        V((slots - 1, 2, D // 8, D), bf16),
        V((extra, 2, D // 8 if n_dp > 8 else 16, D), bf16),
        V((2, D, D), bf16),
        V((SMALL, D), f32),
        V((7, 8, D), f32),
        V((slots, 8, D), f32),
        V((extra, 8, D), f32),
        V((SMALL, D), f32),
        DMA((4,)),
        DMA((1 + G,)),
        DMA((slots - 1, 2, 4)),
        DMA((slots - 1, 2, 4)),
        DMA((slots - 1,)),
        DMA((slots - 1,)),
        DMA((slots, 2, 6)),
        DMA((slots, 2, 6)),
        DMA((extra, 2)),
        DMA((extra, 2)),
        DMA((4, 8)),
        DMA((4, 8)),
    ]
    block_out, input_grad, gr, ge, small = pl.pallas_call(
        functools.partial(kernel, n_dp, n_tensor),
        out_shape=[
            jax.ShapeDtypeStruct((rows, D), bf16),
            jax.ShapeDtypeStruct((rows, D), f32),
            jax.ShapeDtypeStruct((D, D), bf16),
            jax.ShapeDtypeStruct((D, D), bf16),
            jax.ShapeDtypeStruct((SMALL, D), f32),
        ],
        in_specs=[hbm, smem, hbm, vmem, vmem, vmem, vmem, hbm, vmem, hbm, vmem, vmem],
        out_specs=[hbm] * 5,
        scratch_shapes=scratch,
        compiler_params=pltpu.CompilerParams(
            collective_id=0, has_side_effects=True, vmem_limit_bytes=61 << 20
        ),
        cost_estimate=pl.CostEstimate(
            flops=12 * rows * D * D * slots, bytes_accessed=20 * rows * D, transcendentals=0
        ),
    )(
        pixels,
        crop_sides,
        out_cotangent,
        depth_kernel,
        depth_bias.reshape(1, D),
        norm_gain.reshape(1, D),
        norm_shift.reshape(1, D),
        expand_weight,
        expand_bias.reshape(1, D),
        reduce_weight,
        reduce_bias.reshape(1, D),
        layer_scale.reshape(1, D),
    )
    expand_bias_grad = lax.dynamic_slice(
        small, (ROW_EXPAND + lax.axis_index("tensor"), 0), (1, D)
    ).reshape(D)
    return (
        block_out,
        input_grad,
        small[:TAPS],
        small[ROW_BIAS],
        small[ROW_GAIN],
        small[ROW_SHIFT],
        ge.astype(f32),
        expand_bias_grad,
        gr.T.astype(f32),
        small[ROW_REDUCE],
        small[ROW_SCALE],
    )


def solution(mesh):
    in_specs = (
        P(("dp", "tensor"), None),
        P(("dp", "tensor")),
        P(("dp", "tensor"), None),
        P(),
        P(),
        P(),
        P(),
        P(None, "tensor"),
        P("tensor"),
        P("tensor", None),
        P(),
        P(),
    )
    out_specs = (
        P(("dp", "tensor"), None),
        P(("dp", "tensor"), None),
        P(),
        P(),
        P(),
        P(),
        P(None, "tensor"),
        P("tensor"),
        P("tensor", None),
        P(),
        P(),
    )
    return jax.shard_map(
        functools.partial(per_device, mesh.shape["dp"], mesh.shape["tensor"]),
        mesh=mesh,
        in_specs=in_specs,
        out_specs=out_specs,
        check_vma=False,
    )
```

time: 1050 us -> 171 us (0.16)
  waiting for transfers between devices: 533 us -> 0 us
  other arithmetic: 338 us -> 3.01 us
  Pallas kernels: 0 us -> 150 us
  matrix products: 70.9 us -> 0 us
  blocking collectives: 56.6 us -> 0 us
  between operations: 16.2 us -> 0.68 us
  local copies, waits for them, and re-layouts: 29.2 us -> 16.5 us
    reduce_scatter x2 -> x0, waiting for transfers between devices: 276 us -> none  [the longest x1 163 us: per_device(): lax.psum_scatter(jnp.dot(active, reduce_weight, preferred_element_type=jn...]
    reduce_sum x9 -> x0, other arithmetic: 194 us -> none  [the longest x1 91.9 us: front_part(): center = jnp.mean(mixed, axis=1, keepdims=True)]
    all_gather x2 -> x0, waiting for transfers between devices: 179 us -> none  [the longest x1 94.2 us: per_device(): lax.all_gather(normed, 'tensor', axis=0, tiled=True)]
    pallas_call x0 -> x1, Pallas kernels: none -> 150 us  [per_device(): pl.pallas_call(functools.partial(kernel, n_dp, n_tensor), out_shape=[jax....]
    psum x2 -> x0, waiting for transfers between devices: 77.8 us -> none  [the longest x1 77.8 us: per_device(): lax.psum((kernel_grad, depth_bias_grad, gain_grad, shift_grad, reduce_bia...]
    dot_general x6 -> x0, matrix products: 70.9 us -> none  [the longest x2 35.4 us: contract_cols(): lax.dot_general(left_side, right_side, (((1,), (1,)), ((), ())), preferre...]
    add_any x3 -> x0, other arithmetic: 66.3 us -> none  [the longest x2 65.4 us: front_part(): padded[:, offset_row:offset_row + SIDE, offset_col:offset_col + SIDE, :]]
    psum x2 -> x0, blocking collectives: 56.6 us -> none  [the longest x1 41.7 us: per_device(): lax.psum((kernel_grad, depth_bias_grad, gain_grad, shift_grad, reduce_bia...]
  transfers between devices with their start and end apart: 6 -> 0, of which waited for: 5 -> 0; matrix products, arithmetic and copies ran while one was open for 26% -> 0% of each run, Pallas kernels for 0% -> 0%
where the time goes in v1:
time: 171 us; the launch traced here: 170 us
  Pallas kernels  150 us (88%)
  local copies, waits for them, and re-layouts  16.5 us (10%)
  other arithmetic  3.01 us (2%)
    pallas_call x1, Pallas kernels, per_device(): pl.pallas_call(functools.partial(kernel, n_dp, n_tensor), out_shape=[jax....  150 us
    unnamed x9, local copies, waits for them, and re-layouts  5.69 us

profile of v1, /device:TPU:0, one launch (start us, length us, event | category | flops | bytes accessed | tf_op | source)
XLA Modules:
  0.0 170.3 jit_solution(8872144739796872391)
XLA Ops:
  0.6 1.3 reshape.43.depth_bias_ref
  1.9 1.3 reshape.44.gain_ref
  3.2 1.3 reshape.45.shift_ref
  4.4 1.3 reshape.46.eb_ref
  5.7 1.3 reshape.47.rb_ref
  7.0 1.3 reshape.48.scale_ref
  8.2 150.1 %shard_map.203 = (bf16[800,768]{1,0:T(8,128)(2,1)}, f32[800,768]{1,0:T(8,128)}, bf16[768,768]{1,0:T(8,128)(2,1)}, bf16[768,768]{1,0:T(8,128)(2,1)}, f32[64,768]{1,0:T(8,128)}) custom-call(bf16[800,768]{1,0:T(8,128)(2,1)} %pix_hbm.1, s32[8]{0:T(128)} %side_ref.1, bf16[800,768]{1,0:T(8,128)(2,1)} %cot_hbm.1, bf16[49,768]{1,0:T(8,128)(2,1)} %taps_ref.1, ...), custom_call_target="tpu_custom_call" | custom-call | flops 22649241600 | bytes 12288000 | tf_op jit(solution)/shard_map/pallas_call | solution.py:808
  158.3 1.6 slice_reduce_fusion
  160.0 1.6 slice.18
  161.6 1.4 convert_bitcast_fusion
  163.0 0.0 copy-start.2
  163.0 2.0 %copy.23 = f32[768,768]{1,0:T(8,128)} copy(f32[768,768]{0,1:T(8,128)S(1)} %convert_bitcast_fusion) | data formatting | bytes 4718592
  165.0 0.0 copy-done.2
  165.0 0.0 copy-start.1
  165.0 1.6 convert_element_type.9
  166.6 0.2 copy-done.1
  166.7 0.0 copy-start
  166.7 1.0 copy.26
  167.7 1.1 copy-done
  168.9 1.4 copy.27
Async XLA Ops:
  163.0 2.0 %copy-start.2 = (bf16[768,768]{1,0:T(8,128)(2,1)S(1)}, bf16[768,768]{1,0:T(8,128)(2,1)}, u32[]{:S(2)}) copy-start(bf16[768,768]{1,0:T(8,128)(2,1)} %get-tuple-element.19) | copy-start | bytes 3538948
  165.0 1.7 %copy-start.1 = (bf16[800,768]{1,0:T(8,128)(2,1)S(1)}, bf16[800,768]{1,0:T(8,128)(2,1)}, u32[]{:S(2)}) copy-start(bf16[800,768]{1,0:T(8,128)(2,1)} %get-tuple-element.49) | copy-start | bytes 3686404
  166.7 2.1 %copy-start = (f32[800,768]{1,0:T(8,128)S(1)}, f32[800,768]{1,0:T(8,128)}, u32[]{:S(2)}) copy-start(f32[800,768]{1,0:T(8,128)} %get-tuple-element.50) | copy-start | bytes 7372804

commit v2 on v1

--- a/solution.py
+++ b/solution.py
@@ -20,23 +20,35 @@
 MESH = pl.DeviceIdType.MESH
 ROW_BIAS, ROW_GAIN, ROW_SHIFT, ROW_REDUCE, ROW_SCALE, ROW_EXPAND = 49, 50, 51, 52, 53, 54
 SMALL = 64
+PLAN = (
+    "W0.0.0", "taps", "pix", "W0.0.1", "conv:0", "W1.2.0", "W1.1.1", "W1.1.0", "conv:1", "W1.2.1",
+    "conv:2", "conv:3", "W2.1.1", "conv:4", "W2.1.0", "conv:5", "W1.3.1", "cot", "ln:0", "ln:1",
+    "ln:2", "W1.3.0", "ln:3", "h:0:0", "h:0:1", "W2.2.1", "W3.1.0", "W3.1.1", "W2.2.0", "h:0:2",
+    "h:0:3", "h:1:0", "gr:0:0", "W2.3.1", "gr:0:1", "W2.3.0", "h:1:1", "h:1:2", "gr:0:2", "h:1:3",
+    "W3.2.1", "gr:1:0", "W3.2.0", "gr:1:1", "gr:1:2", "G0.1.0", "G0.1.1", "h:2:0", "h:2:1",
+    "G1.1.0", "h:2:2", "h:2:3", "W3.3.1", "G1.1.1", "W3.3.0", "gr:2:0", "gr:2:1", "gr:2:2",
+    "G0.2.0", "G0.2.1", "h:3:0", "h:3:1", "h:3:2", "G1.2.1", "G1.2.0", "h:3:3", "ncot", "G0.0.0",
+    "G2.1.1", "G2.1.0", "lnb:0", "gr:3:0", "G2.2.0", "gr:3:1", "G2.2.1", "gr:3:2", "G0.3.0",
+    "G0.3.1", "lnb:1", "G0.0.1", "G1.3.0", "G1.3.1", "kg:0", "G3.2.0", "kg:1", "kg:2", "G1.0.0",
+    "G3.2.1", "kg:3", "G3.1.1", "G3.1.0", "kg:4", "kg:5", "G2.3.0", "branch", "G1.0.1", "G2.3.1",
+    "bout", "G3.3.0", "small", "G2.0.0", "convb:0", "S0", "G3.3.1", "G2.0.1", "S1", "convb:1",
+    "A0.0", "S2", "A0.1", "S3", "A1.0", "A1.1", "convb:2", "convb:3", "convb:4", "convb:5", "A2.0",
+    "A2.1",
+)
 
 
 def gelu_both(h):
-    a = jnp.abs(h)
-    t = 1.0 / (1.0 + a * (0.3275911 / math.sqrt(2.0)))
-    e = jnp.exp(h * h * -0.5)
-    poly = t * (
-        0.254829592
-        + t * (-0.284496736 + t * (1.421413741 + t * (-1.453152027 + t * 1.061405429)))
-    )
-    q = 0.5 * e * poly
-    phi = jnp.where(h >= 0.0, 1.0 - q, q)
-    return h * phi, phi + h * (e * (1.0 / math.sqrt(2.0 * math.pi)))
+    phi = 0.5 + 0.5 * lax.erf(h * math.sqrt(0.5))
+    bell = jnp.exp2(h * h * (-0.5 * math.log2(math.e)))
+    return h * phi, phi + h * (1.0 / math.sqrt(2.0 * math.pi)) * bell
 
 
 def dot(a, b):
     return jnp.dot(a, b, preferred_element_type=f32)
+
+
+def dot_rows(a, b):
+    return lax.dot_general(a, b, (((0,), (0,)), ((), ())), preferred_element_type=f32)
 
 
 def dot_t(a, b):
@@ -71,8 +83,6 @@
     CM,
     BC,
     KB,
-    NT,
-    BT,
     WE,
     WR,
     EB,
@@ -133,7 +143,15 @@
                 d = d + (1 - 2 * bits[b]) * (1 << b)
         return d
 
-    OFF = [0, 1, n_tensor - 1] + list(range(2, n_tensor - 1))
+
+    t_low = lax.rem(tz, 2)
+    t_high = lax.div(tz, 2)
+    partner = tz + 1 - 2 * t_low
+    middle = t_low + t_high - 2 * t_low * t_high
+    across = 3 - tz
+
+    def shard_of(s):
+        return (tz, partner, 2 - t_high, 3 - 3 * t_high)[s]
 
     peers = [(flip_low(j), tz) for j in range(1, 8)]
     peers += [(dp, lax.rem(tz + o, n_tensor)) for o in range(1, n_tensor)]
@@ -151,6 +169,9 @@
     for copy in loads:
         copy.start()
 
+    def vector(ref):
+        return ref[...].astype(f32).reshape(1, D)
+
     def remote(src, dst, send, recv, device):
         return pltpu.make_async_remote_copy(
             src_ref=src, dst_ref=dst, send_sem=send, recv_sem=recv,
@@ -173,38 +194,53 @@
         return pl.ds(pl.multiple_of(start, 16), size)
 
     def w_copy(s, m, level):
-        rows = w_rows(m, level)
-        here = W[m].at[s, rows, :]
-        src = here
+        here = W[m].at[s, w_rows(m, level), :]
+        device = ((first_peer[m], tz), (second_peer[m], tz), (flip(0), tz))[level - 1]
+        return remote(here, here, w_send.at[s, m, level], w_recv.at[s, m, level], device)
+
+    def z_piece(m, source, slot, device):
+        rows = w_rows(m, 0)
+        src = (we_hbm, wr_hbm)[m].at[rows, :] if source == 0 else W[m].at[source, rows, :]
+        send = w_send.at[0, m, slot] if source == 0 else w_send.at[source, m, 0]
+        return remote(src, W[m].at[slot, rows, :], send, w_recv.at[slot, m, 0], (dp, device))
+
+    def own_pieces(m):
+        return z_piece(m, 0, 1, partner), z_piece(m, 0, 2, across)
+
+    def relay(s, m):
+        return z_piece(m, 1, 3, across) if s == 1 else z_piece(m, s, s, partner)
+
+    def in_middle(act):
+        @pl.when(middle == 1)
+        def _():
+            act()
+
+    def e_copy(o):
+        own = EB.at[tz]
+        return remote(own, own, e_send.at[o], e_recv.at[tz], (dp, lax.rem(tz + o, n_tensor)))
+
+    def e_arrival(s):
+        there = EB.at[shard_of(s)]
+        return remote(there, there, e_send.at[s], e_recv.at[shard_of(s)], (dp, partner))
+
+    def w_step(level, s, m):
         if level == 0:
-            src = (we_hbm, wr_hbm)[m].at[rows, :]
-            device = (dp, lax.rem(tz + n_tensor - OFF[s], n_tensor))
-        elif level == 1:
-            device = (first_peer[m], tz)
-        elif level == 2:
-            device = (second_peer[m], tz)
+            to_partner, to_other = own_pieces(m)
+            to_partner.start()
+            in_middle(to_other.start)
+            return
+        if level == 1:
+            z_piece(m, 0, s, partner).wait_recv()
+            in_middle(relay(s, m).start)
         else:
-            device = (flip(0), tz)
-        return remote(src, here, w_send.at[s - 1, m, level], w_recv.at[s - 1, m, level], device)
-
-    def e_copy(s):
-        device = (dp, lax.rem(tz + n_tensor - OFF[s], n_tensor))
-        return remote(EB.at[0], EB.at[s], e_send.at[s - 1], e_recv.at[s - 1], device)
-
-    def w_step(s, level):
-        for m in range(2):
-            if level > 0:
-                w_copy(s, m, level - 1).wait_recv()
-            if level < 4:
-                w_copy(s, m, level).start()
-        if level == 4:
-            e_copy(s).wait_recv()
-
-    EB[0] = jnp.broadcast_to(eb_ref[...].astype(f32), (8, D))
+            w_copy(s, m, level - 1).wait_recv()
+        if level < 4:
+            w_copy(s, m, level).start()
+
+    EB[tz] = jnp.broadcast_to(vector(eb_ref), (8, D))
     pl.semaphore_wait(barrier, len(peers))
-    for s in range(1, SLOTS):
-        w_step(s, 0)
-        e_copy(s).start()
+    for o in range(1, n_tensor):
+        e_copy(o).start()
 
     g_first = (yb, xb)
     g_second = (xb, yb)
@@ -235,29 +271,34 @@
 
     def z_copy(s, m):
         src = GS.at[s, m, pl.ds(pl.multiple_of(g_start(m, 2), 16), PIECE), :]
-        device = (dp, lax.rem(tz + OFF[s], n_tensor))
-        return remote(src, RZ.at[s - 1, m], g_send.at[s, m, 3], g_recv.at[s, m, 3], device)
-
-    def g_step(s, level):
-        for m in range(2):
-            if level > 0:
-                g_copy(s, m, level - 1).wait_recv()
-                got = (R0, R1, R2)[level - 1]
-                start = g_start(m, level - 1)
-                size = (HALF, QUART, PIECE)[level - 1]
-
-                def add(i, c):
-                    rows = pl.ds(pl.multiple_of(start + i * 16, 16), 16)
-                    GS[s, m, rows, :] = (
-                        GS[s, m, rows, :] + got[s, m, pl.ds(pl.multiple_of(i * 16, 16), 16), :]
-                    )
-                    return c
-
-                lax.fori_loop(0, size // 16, add, 0)
-            if level < 3:
-                g_copy(s, m, level).start()
-            elif s > 0:
-                z_copy(s, m).start()
+        slot = 1 if s == 1 else 3 - middle
+        return remote(
+            src, RZ.at[slot - 1, m], g_send.at[s, m, 3], g_recv.at[slot, m, 3], (dp, shard_of(s))
+        )
+
+    def z_arrival(s, m):
+        src = GS.at[s, m, pl.ds(pl.multiple_of(g_start(m, 2), 16), PIECE), :]
+        return remote(src, RZ.at[s - 1, m], g_send.at[s, m, 3], g_recv.at[s, m, 3], (dp, partner))
+
+    def g_step(level, s, m):
+        if level > 0:
+            g_copy(s, m, level - 1).wait_recv()
+            got = (R0, R1, R2)[level - 1]
+            start = g_start(m, level - 1)
+            size = (HALF, QUART, PIECE)[level - 1]
+
+            def add(i, c):
+                rows = pl.ds(pl.multiple_of(start + i * 16, 16), 16)
+                GS[s, m, rows, :] = (
+                    GS[s, m, rows, :] + got[s, m, pl.ds(pl.multiple_of(i * 16, 16), 16), :]
+                )
+                return c
+
+            lax.fori_loop(0, size // 16, add, 0, unroll=2)
+        if level < 3:
+            g_copy(s, m, level).start()
+        elif s > 0:
+            z_copy(s, m).start()
 
     def a_copy(m, level):
         if level == 0:
@@ -273,41 +314,42 @@
         here = OUTB.at[m, pl.ds(pl.multiple_of(g_start(m, 2), 16), PIECE), :]
         return remote(here, RX.at[b - 3, m], x_send.at[b - 3, m], x_recv.at[b - 3, m], (flip(b), tz))
 
-    def finish_sum():
-        for m in range(2):
+    def finish_sum(m):
+        g_step(3, 0, m)
+        for s in range(1, SLOTS):
+            z_arrival(s, m).wait_recv()
+        start = g_start(m, 2)
+
+        def add(i, c):
+            rows = pl.ds(pl.multiple_of(start + i * 16, 16), 16)
+            own = pl.ds(pl.multiple_of(i * 16, 16), 16)
+            total = GS[0, m, rows, :].astype(f32)
             for s in range(1, SLOTS):
-                z_copy(s, m).wait_recv()
-            start = g_start(m, 2)
-
-            def add(i, c):
+                total = total + RZ[s - 1, m, own, :].astype(f32)
+            OUTB[m, rows, :] = total.astype(bf16)
+            return c
+
+        lax.fori_loop(0, PIECE // 16, add, 0)
+        for b in range(3, 3 + extra):
+            x_copy(m, b).start()
+            x_copy(m, b).wait()
+
+            def add_x(i, c):
                 rows = pl.ds(pl.multiple_of(start + i * 16, 16), 16)
-                own = pl.ds(pl.multiple_of(i * 16, 16), 16)
-                total = GS[0, m, rows, :].astype(f32)
-                for s in range(1, SLOTS):
-                    total = total + RZ[s - 1, m, own, :].astype(f32)
-                OUTB[m, rows, :] = total.astype(bf16)
+                OUTB[m, rows, :] = (
+                    OUTB[m, rows, :] + RX[b - 3, m, pl.ds(pl.multiple_of(i * 16, 16), 16), :]
+                )
                 return c
 
-            lax.fori_loop(0, PIECE // 16, add, 0)
-            for b in range(3, 3 + extra):
-                x_copy(m, b).start()
-                x_copy(m, b).wait()
-
-                def add_x(i, c):
-                    rows = pl.ds(pl.multiple_of(start + i * 16, 16), 16)
-                    OUTB[m, rows, :] = (
-                        OUTB[m, rows, :] + RX[b - 3, m, pl.ds(pl.multiple_of(i * 16, 16), 16), :]
-                    )
-                    return c
-
-                lax.fori_loop(0, PIECE // 16, add_x, 0)
-            a_copy(m, 0).start()
-
-    def a_step(level):
-        for m in range(2):
+            lax.fori_loop(0, PIECE // 16, add_x, 0)
+
+    def a_step(level, m):
+        if level == 0:
+            finish_sum(m)
+        else:
             a_copy(m, level - 1).wait_recv()
-            if level < 3:
-                a_copy(m, level).start()
+        if level < 3:
+            a_copy(m, level).start()
 
     def sr_copy(j):
         dst_low = flip_low(j)
@@ -396,7 +438,7 @@
         lax.fori_loop(0, PLACES, body, 0, unroll=2)
 
     def load_cot():
-        scale = scale_ref[...].astype(f32)
+        scale = vector(scale_ref)
 
         def body(q, sums):
             sums = list(sums)
@@ -448,9 +490,9 @@
 
         lax.fori_loop(0, G, one, 0)
 
-    def layernorm():
-        gain = gain_ref[...].astype(f32)
-        shift = shift_ref[...].astype(f32)
+    def layernorm(lo, hi):
+        gain = vector(gain_ref)
+        shift = vector(shift_ref)
 
         def body(q, c):
             rows = pl.ds(pl.multiple_of(q * 16, 16), 16)
@@ -467,10 +509,10 @@
                 NM[rows, lanes(g)] = (xh * gain[:, lanes(g)] + shift[:, lanes(g)]).astype(bf16)
             return c
 
-        lax.fori_loop(0, ROWS // 16, body, 0, unroll=2)
-
-    def layernorm_back():
-        gain = gain_ref[...].astype(f32)
+        lax.fori_loop(lo, hi, body, 0, unroll=5)
+
+    def layernorm_back(lo, hi):
+        gain = vector(gain_ref)
 
         def body(q, sums):
             gains, shifts, biases = [list(part) for part in sums]
@@ -493,12 +535,12 @@
             return tuple(gains), tuple(shifts), tuple(biases)
 
         zeros = (jnp.zeros((8, LANES), f32),) * G
-        sums = lax.fori_loop(0, ROWS // 16, body, (zeros, zeros, zeros))
+        sums = lax.fori_loop(lo, hi, body, (zeros, zeros, zeros), unroll=5)
         for i in range(3):
             for g in range(G):
-                ACC[i, g] = sums[i][g]
-
-    def kernel_grad():
+                ACC[i, g] = sums[i][g] if lo == 0 else ACC[i, g] + sums[i][g]
+
+    def kernel_grad(between):
         def one(g, carry):
             for dr in range(KERNEL):
                 acc = [[None, None] for _ in range(KERNEL)]
@@ -516,42 +558,45 @@
                                 v = ds[c] * xs[cc]
                                 a[c % 2] = v if a[c % 2] is None else a[c % 2] + v
                 for dc in range(KERNEL):
-                    KG[g, place(dr * KERNEL + dc), :] = acc[dc][0] + acc[dc][1]
+                    t = dr * KERNEL + dc
+                    KG[g, t : t + 1, :] = jnp.sum(acc[dc][0] + acc[dc][1], axis=0, keepdims=True)
+            between(g)
             return carry
 
         lax.fori_loop(0, G, one, 0)
 
     def hidden_block(s, j):
-        cols = slice(j * BLOCK, (j + 1) * BLOCK)
-        h = dot(NM[...], WE[s, :, cols])
-        stage[0] = h[:, :LANES]
-        stage[1] = h[:, LANES:]
-        a = dot_t(BC[...], WR[s, cols, :])
-        stage[2] = a[:, :LANES]
-        stage[3] = a[:, LANES:]
-
-        def body(i, sums):
-            rows = pl.ds(pl.multiple_of(i * 16, 16), 16)
-            out = []
+        if j < D // BLOCK:
+            cols = slice(j * BLOCK, (j + 1) * BLOCK)
+            base = j % 2 * 4
+            h = dot(NM[...], WE[s, :, cols])
+            stage[base] = h[:, :LANES]
+            stage[base + 1] = h[:, LANES:]
+            a = dot_t(BC[...], WR[s, cols, :])
+            stage[base + 2] = a[:, :LANES]
+            stage[base + 3] = a[:, LANES:]
+        if j > 0:
+            base = (j - 1) % 2 * 4
             for u in range(2):
-                mine = slice(j * BLOCK + u * LANES, j * BLOCK + (u + 1) * LANES)
-                value, slope = gelu_both(stage[u, rows, :] + EB[s, 0:1, mine])
-                ACT[s, rows, mine] = value.astype(bf16)
-                w = (stage[2 + u, rows, :] * slope).astype(bf16)
-                HC[s, rows, mine] = w
-                w = w.astype(f32)
-                out.append(sums[u] + (w[:8] + w[8:]))
-            return tuple(out)
-
-        zero = jnp.zeros((8, LANES), f32)
-        sums = lax.fori_loop(0, ROWS // 16, body, (zero, zero), unroll=5)
-        for u in range(2):
-            EBG[s, :, j * BLOCK + u * LANES : j * BLOCK + (u + 1) * LANES] = sums[u]
+                mine = slice((j - 1) * BLOCK + u * LANES, (j - 1) * BLOCK + (u + 1) * LANES)
+                bias = EB[shard_of(s), :, mine]
+                bias = jnp.concatenate([bias, bias], axis=0)
+                total = None
+                for i in range(ROWS // 16):
+                    rows = slice(i * 16, (i + 1) * 16)
+                    value, slope = gelu_both(stage[base + u, rows, :] + bias)
+                    ACT[s, rows, mine] = value.astype(bf16)
+                    w = (stage[base + 2 + u, rows, :] * slope).astype(bf16)
+                    HC[s, rows, mine] = w
+                    w = w.astype(f32)
+                    w = w[:8] + w[8:]
+                    total = w if total is None else total + w
+                EBG[s, :, mine] = total
 
     def grad_block(s, j):
         cols = slice(j * BLOCK, (j + 1) * BLOCK)
-        GS[s, 0, :, cols] = dot(BT[...], ACT[s, :, cols]).astype(bf16)
-        GS[s, 1, :, cols] = dot(NT[...], HC[s, :, cols]).astype(bf16)
+        GS[s, 0, cols, :] = dot_rows(ACT[s, :, cols], BC[...]).astype(bf16)
+        GS[s, 1, :, cols] = dot_rows(NM[...], HC[s, :, cols]).astype(bf16)
 
     def back_to_normed():
         for n in range(D // BLOCK):
@@ -572,8 +617,8 @@
             XH[2 * n + 1] = total[:, LANES:]
 
     def block_output():
-        scale = scale_ref[...].astype(f32)
-        shift = rb_ref[...].astype(f32)
+        scale = vector(scale_ref)
+        shift = vector(rb_ref)
 
         def body(q, sums):
             sums = list(sums)
@@ -604,74 +649,29 @@
     def small_sums():
         S[...] = jnp.zeros_like(S)
         for g in range(G):
-            for t in range(TAPS):
-                S[t : t + 1, lanes(g)] = jnp.sum(KG[g, place(t), :], axis=0, keepdims=True)
+            S[:TAPS, lanes(g)] = KG[g, :TAPS, :]
             for r, i in ((ROW_BIAS, 2), (ROW_GAIN, 0), (ROW_SHIFT, 1), (ROW_REDUCE, 3), (ROW_SCALE, 4)):
                 S[r : r + 1, lanes(g)] = jnp.sum(ACC[i, g], axis=0, keepdims=True)
         for s in range(SLOTS):
-            r = ROW_EXPAND + lax.rem(tz + OFF[s], n_tensor)
+            r = ROW_EXPAND + shard_of(s)
             S[pl.ds(r, 1), :] = jnp.sum(EBG[s], axis=0, keepdims=True)
 
+    def tell(name):
+        kind, _, rest = name.partition(".")
+        where = [int(v) for v in rest.split(".")] if rest else []
+        if kind[0] == "W":
+            w_step(int(kind[1]), *where)
+        elif kind[0] == "G":
+            g_step(int(kind[1]), *where)
+        elif kind[0] == "A":
+            a_step(int(kind[1]), *where)
+        else:
+            small_step(int(kind[1]))
+
     loads[0].wait()
-    spread(NM)
-    load_pixels()
-    load_taps()
-    w_plan = [[(1, 1)], [(2, 1), (1, 2)], [(1, 3)], [(2, 2)], [(3, 1)], [(2, 3), (1, 4)]]
-
-    def during_conv(g):
-        for i in range(G):
-            @pl.when(g == i)
-            def _():
-                for s, level in w_plan[i] if i < len(w_plan) else []:
-                    w_step(s, level)
-
-    biases = depth_bias_ref[...].astype(f32)
+    biases = vector(depth_bias_ref)
     for g in range(G):
         ACC[0, g] = jnp.broadcast_to(biases[:, lanes(g)], (8, LANES))
-    conv(X, XH, ACC.at[0], False, None, during_conv)
-    loads[1].wait()
-    spread(BC)
-    load_cot()
-    layernorm()
-    w_step(3, 2)
-    NT[...] = NM[...].T
-    BT[...] = BC[...].T
-    loads[2].wait()
-    loads[3].wait()
-    for s in range(SLOTS):
-        if s == 2:
-            w_step(2, 4)
-        if s == 3:
-            w_step(3, 4)
-        for j in range(D // BLOCK):
-            hidden_block(s, j)
-            if s == 0 and j == 0:
-                w_step(3, 3)
-            if s > 0 and j == 0:
-                g_step(s - 1, 1)
-            if s > 1 and j == 1:
-                g_step(s - 2, 3)
-        for j in range(D // BLOCK):
-            grad_block(s, j)
-        g_step(s, 0)
-        if s > 0:
-            g_step(s - 1, 2)
-    last = SLOTS - 1
-    back_to_normed()
-    g_step(last, 1)
-    g_step(last - 1, 3)
-    layernorm_back()
-    g_step(last, 2)
-    kernel_grad()
-    g_step(last, 3)
-    to_branch()
-    finish_sum()
-    block_output()
-    pltpu.make_async_copy(NM, out_hbm, out_sem.at[0]).start()
-    small_sums()
-    small_step(0)
-    a_step(1)
-    small_step(1)
 
     def finish_input(g, r, acc):
         cols = pl.ds(pl.multiple_of(g * LANES, LANES), LANES)
@@ -688,20 +688,95 @@
             XH.at[g], in_grad_hbm.at[:, pl.ds(pl.multiple_of(g * LANES, LANES), LANES)], out_sem.at[1 + g]
         )
 
-    def during_back(g):
-        out_copy(g).start()
-
-        @pl.when(g == 1)
-        def _():
-            a_step(2)
-            small_step(2)
-
-        @pl.when(g == 4)
-        def _():
-            a_step(3)
-
-    conv(NC, None, None, True, finish_input, during_back)
-    small_step(3)
+    def over_groups(names, call):
+        kind = names[0].partition(":")[0]
+        after = {}
+        group = 0
+        for name in names:
+            if name.startswith(kind + ":"):
+                group = int(name.partition(":")[2])
+            else:
+                after.setdefault(group, []).append(name)
+
+        def between(g):
+            if kind == "convb":
+                out_copy(g).start()
+            for i, told in after.items():
+                @pl.when(g == i)
+                def _():
+                    for name in told:
+                        tell(name)
+
+        call(between)
+
+    looped = {
+        "conv": lambda between: conv(X, XH, ACC.at[0], False, None, between),
+        "kg": kernel_grad,
+        "convb": lambda between: conv(NC, None, None, True, finish_input, between),
+    }
+
+    def start_output():
+        block_output()
+        pltpu.make_async_copy(NM, out_hbm, out_sem.at[0]).start()
+
+    def pixels_in():
+        spread(NM)
+        load_pixels()
+
+    def cot_in():
+        loads[1].wait()
+        spread(BC)
+        load_cot()
+
+    def linears_ready(s):
+        if s == 0:
+            loads[2].wait()
+            loads[3].wait()
+        else:
+            for m in range(2):
+                w_step(4, s, m)
+            e_arrival(s).wait_recv()
+
+    def step(name):
+        kind, _, rest = name.partition(":")
+        where = [int(v) for v in rest.split(":")] if rest else []
+        if "." in name or kind[0] == "S":
+            tell(name)
+        elif kind == "ln":
+            n = ROWS // 16
+            layernorm(n * where[0] // 20 * 5, n * (where[0] + 1) // 20 * 5)
+        elif kind == "lnb":
+            n = ROWS // 16
+            layernorm_back(n * where[0] // 2, n * (where[0] + 1) // 2)
+        elif kind == "h":
+            if where[1] == 0:
+                linears_ready(where[0])
+            hidden_block(*where)
+        elif kind == "gr":
+            grad_block(*where)
+        else:
+            {
+                "pix": pixels_in,
+                "taps": load_taps,
+                "cot": cot_in,
+                "ncot": back_to_normed,
+                "branch": to_branch,
+                "bout": start_output,
+                "small": small_sums,
+            }[kind]()
+
+    at = 0
+    while at < len(PLAN):
+        kind = PLAN[at].partition(":")[0]
+        if kind in looped:
+            last = max(i for i, name in enumerate(PLAN) if name.startswith(kind + ":"))
+            over_groups(PLAN[at : last + 1], looped[kind])
+            at = last + 1
+        else:
+            step(PLAN[at])
+            at += 1
+    for m in range(2):
+        a_step(3, m)
     tail = [
         pltpu.make_async_copy(OUTB.at[0], gr_hbm, load_sem.at[0]),
         pltpu.make_async_copy(OUTB.at[1], ge_hbm, load_sem.at[1]),
@@ -709,10 +784,14 @@
     ]
     for copy in tail:
         copy.start()
+    for m in range(2):
+        own_pieces(m)[0].wait_send()
+        in_middle(own_pieces(m)[1].wait_send)
     for s in range(1, SLOTS):
         e_copy(s).wait_send()
         for m in range(2):
-            for level in range(4):
+            in_middle(relay(s, m).wait_send)
+            for level in range(1, 4):
                 w_copy(s, m, level).wait_send()
             z_copy(s, m).wait_send()
     for s in range(SLOTS):
@@ -731,6 +810,61 @@
     for g in range(G):
         out_copy(g).wait()
     for copy in tail:
+        copy.wait()
+
+
+def hand_over(
+    out_in, grad_in, gr, ge, small,
+    block_out, input_grad, kernel_grad, bias_grad, gain_grad, shift_grad,
+    expand_grad, expand_bias_grad, reduce_grad, reduce_bias_grad, scale_grad,
+    narrow, wide, whole_sem, in_sem, out_sem,
+):
+    D = gr.shape[0]
+    third = D // 3
+    whole = [
+        pltpu.make_async_copy(grad_in, input_grad, whole_sem.at[0]),
+        pltpu.make_async_copy(out_in, block_out, whole_sem.at[1]),
+    ]
+    parts = [(i, m) for i in range(3) for m in range(2)]
+
+    def rows(i):
+        return pl.ds(i * third, third)
+
+    reads = {
+        (i, m): pltpu.make_async_copy((gr, ge)[m].at[rows(i)], narrow.at[m, rows(i)], in_sem.at[m, i])
+        for i, m in parts
+    }
+    writes = {
+        (i, m): pltpu.make_async_copy(
+            wide.at[m, rows(i)], (reduce_grad, expand_grad)[m].at[rows(i)], out_sem.at[m, i]
+        )
+        for i, m in parts
+    }
+    for part in parts:
+        reads[part].start()
+    for copy in whole:
+        copy.start()
+    kernel_grad[...] = small[:TAPS, :]
+    own = ROW_EXPAND + lax.axis_index("tensor")
+    for row, ref in (
+        (ROW_BIAS, bias_grad), (ROW_GAIN, gain_grad), (ROW_SHIFT, shift_grad),
+        (ROW_REDUCE, reduce_bias_grad), (ROW_SCALE, scale_grad),
+    ):
+        ref[...] = small[row : row + 1, :].reshape(D)
+    expand_bias_grad[...] = small[pl.ds(own, 1), :].reshape(D)
+    for i, m in parts:
+        reads[i, m].wait()
+
+        def widen(k, c):
+            at = pl.ds(pl.multiple_of(i * third + k * 32, 32), 32)
+            wide[m, at, :] = narrow[m, at, :].astype(f32)
+            return c
+
+        lax.fori_loop(0, third // 32, widen, 0)
+        writes[i, m].start()
+    for part in parts:
+        writes[part].wait()
+    for copy in whole:
         copy.wait()
 
 
@@ -756,12 +890,12 @@
     slots = n_tensor
     extra = max(n_dp.bit_length() - 4, 1)
     vmem = pl.BlockSpec(memory_space=pltpu.VMEM)
-    hbm = pl.BlockSpec(memory_space=pl.ANY)
+    hbm = pl.BlockSpec(memory_space=pltpu.HBM)
     smem = pl.BlockSpec(memory_space=pltpu.SMEM)
     V = pltpu.VMEM
     DMA = pltpu.SemaphoreType.DMA
     scratch = [
-        V((G, rows, LANES), f32),
+        V((8, rows, LANES), f32),
         V((G, rows, LANES), f32),
         V((G, rows, LANES), f32),
         V((rows, LANES), f32),
@@ -769,8 +903,6 @@
         V((rows, D), bf16),
         V((rows, D), bf16),
         V((G, TAPS * img, LANES), f32),
-        V((D, rows), bf16),
-        V((D, rows), bf16),
         V((slots, D, D), bf16),
         V((slots, D, D), bf16),
         V((slots, 8, D), f32),
@@ -778,7 +910,7 @@
         V((slots, rows, D), bf16),
         V((slots, 8, D), f32),
         V((G, rows, LANES), f32),
-        V((G, TAPS * img, LANES), f32),
+        V((G, 56, LANES), f32),
         V((5, G, 8, LANES), f32),
         V((slots, 2, D, D), bf16),
         V((slots, 2, D // 2, D), bf16),
@@ -794,10 +926,10 @@
         V((SMALL, D), f32),
         DMA((4,)),
         DMA((1 + G,)),
-        DMA((slots - 1, 2, 4)),
-        DMA((slots - 1, 2, 4)),
-        DMA((slots - 1,)),
-        DMA((slots - 1,)),
+        DMA((slots, 2, 4)),
+        DMA((slots, 2, 4)),
+        DMA((slots,)),
+        DMA((slots,)),
         DMA((slots, 2, 6)),
         DMA((slots, 2, 6)),
         DMA((extra, 2)),
@@ -828,31 +960,36 @@
         crop_sides,
         out_cotangent,
         depth_kernel,
-        depth_bias.reshape(1, D),
-        norm_gain.reshape(1, D),
-        norm_shift.reshape(1, D),
+        depth_bias,
+        norm_gain,
+        norm_shift,
         expand_weight,
-        expand_bias.reshape(1, D),
+        expand_bias,
         reduce_weight,
-        reduce_bias.reshape(1, D),
-        layer_scale.reshape(1, D),
+        reduce_bias,
+        layer_scale,
     )
-    expand_bias_grad = lax.dynamic_slice(
-        small, (ROW_EXPAND + lax.axis_index("tensor"), 0), (1, D)
-    ).reshape(D)
-    return (
-        block_out,
-        input_grad,
-        small[:TAPS],
-        small[ROW_BIAS],
-        small[ROW_GAIN],
-        small[ROW_SHIFT],
-        ge.astype(f32),
-        expand_bias_grad,
-        gr.T.astype(f32),
-        small[ROW_REDUCE],
-        small[ROW_SCALE],
-    )
+    vec = jax.ShapeDtypeStruct((D,), f32)
+    square = jax.ShapeDtypeStruct((D, D), f32)
+    return pl.pallas_call(
+        hand_over,
+        out_shape=[
+            jax.ShapeDtypeStruct((rows, D), bf16),
+            jax.ShapeDtypeStruct((rows, D), f32),
+            jax.ShapeDtypeStruct((TAPS, D), f32),
+            vec, vec, vec, square, vec, square, vec, vec,
+        ],
+        in_specs=[hbm, hbm, hbm, hbm, vmem],
+        out_specs=[hbm, hbm, vmem, vmem, vmem, vmem, hbm, vmem, hbm, vmem, vmem],
+        scratch_shapes=[
+            V((2, D, D), bf16),
+            V((2, D, D), f32),
+            DMA((2,)),
+            DMA((2, 3)),
+            DMA((2, 3)),
+        ],
+        compiler_params=pltpu.CompilerParams(vmem_limit_bytes=60 << 20),
+    )(block_out, input_grad, gr, ge, small)
 
 
 def solution(mesh):

time: 171 us -> 237 us (1.39)
  Pallas kernels: 150 us -> 236 us
  local copies, waits for them, and re-layouts: 16.5 us -> 0 us
  other arithmetic: 3.01 us -> 0 us
    pallas_call x0 -> x1, Pallas kernels: none -> 115 us  [per_device(): pl.pallas_call(hand_over, out_shape=[jax.ShapeDtypeStruct((rows, D), bf16...]
    pallas_call x1, Pallas kernels: 150 us -> 121 us  [per_device(): pl.pallas_call(functools.partial(kernel, n_dp, n_tensor), out_shape=[jax....]
    reshape x6 -> x0, local copies, waits for them, and re-layouts: 7.57 us -> none  [the longest x1 1.26 us: per_device(): depth_bias.reshape(1, D)]
    unnamed x9 -> x0, local copies, waits for them, and re-layouts: 5.69 us -> none
    slice x2 -> x0, local copies, waits for them, and re-layouts: 3.22 us -> none  [the longest x1 1.62 us: per_device(): small[ROW_SCALE]]
    convert_element_type x2 -> x0, other arithmetic: 3.01 us -> none  [the longest x1 1.58 us: per_device(): ge.astype(f32)]
where the time goes in v2:
time: 237 us
  Pallas kernels  236 us (100%)
    pallas_call x1, Pallas kernels, per_device(): pl.pallas_call(functools.partial(kernel, n_dp, n_tensor), out_shape=[jax....  121 us
    pallas_call x1, Pallas kernels, per_device(): pl.pallas_call(hand_over, out_shape=[jax.ShapeDtypeStruct((rows, D), bf16...  115 us

profile of v2, /device:TPU:0, one launch (start us, length us, event | category | flops | bytes accessed | tf_op | source)
XLA Modules:
  0.0 236.6 jit_solution(726686367527988707)
XLA Ops:
  0.6 121.2 %shard_map.203 = (bf16[800,768]{1,0:T(8,128)(2,1)}, f32[800,768]{1,0:T(8,128)}, bf16[768,768]{1,0:T(8,128)(2,1)}, bf16[768,768]{1,0:T(8,128)(2,1)}, f32[64,768]{1,0:T(8,128)}) custom-call(bf16[800,768]{1,0:T(8,128)(2,1)} %pix_hbm.1, s32[8]{0:T(128)} %side_ref.1, bf16[800,768]{1,0:T(8,128)(2,1)} %cot_hbm.1, bf16[49,768]{1,0:T(8,128)(2,1)} %taps_ref.1, ...), custom_call_target="tpu_custom_call" | custom-call | flops 22649241600 | bytes 12288000 | tf_op jit(solution)/shard_map/pallas_call | solution.py:940
  121.9 114.5 %shard_map.204 = (bf16[800,768]{1,0:T(8,128)(2,1)}, f32[800,768]{1,0:T(8,128)}, f32[49,768]{1,0:T(8,128)}, f32[768]{0:T(1024)}, f32[768]{0:T(1024)}, /*index=5*/...) custom-call(bf16[800,768]{1,0:T(8,128)(2,1)} %get-tuple-element.16.o, ...), custom_call_target="tpu_custom_call" | custom-call | tf_op jit(solution)/shard_map/pallas_call | solution.py:974

commit v3 on v2

--- a/solution.py
+++ b/solution.py
@@ -21,19 +21,18 @@
 ROW_BIAS, ROW_GAIN, ROW_SHIFT, ROW_REDUCE, ROW_SCALE, ROW_EXPAND = 49, 50, 51, 52, 53, 54
 SMALL = 64
 PLAN = (
-    "W0.0.0", "taps", "pix", "W0.0.1", "conv:0", "W1.2.0", "W1.1.1", "W1.1.0", "conv:1", "W1.2.1",
-    "conv:2", "conv:3", "W2.1.1", "conv:4", "W2.1.0", "conv:5", "W1.3.1", "cot", "ln:0", "ln:1",
-    "ln:2", "W1.3.0", "ln:3", "h:0:0", "h:0:1", "W2.2.1", "W3.1.0", "W3.1.1", "W2.2.0", "h:0:2",
-    "h:0:3", "h:1:0", "gr:0:0", "W2.3.1", "gr:0:1", "W2.3.0", "h:1:1", "h:1:2", "gr:0:2", "h:1:3",
-    "W3.2.1", "gr:1:0", "W3.2.0", "gr:1:1", "gr:1:2", "G0.1.0", "G0.1.1", "h:2:0", "h:2:1",
-    "G1.1.0", "h:2:2", "h:2:3", "W3.3.1", "G1.1.1", "W3.3.0", "gr:2:0", "gr:2:1", "gr:2:2",
-    "G0.2.0", "G0.2.1", "h:3:0", "h:3:1", "h:3:2", "G1.2.1", "G1.2.0", "h:3:3", "ncot", "G0.0.0",
-    "G2.1.1", "G2.1.0", "lnb:0", "gr:3:0", "G2.2.0", "gr:3:1", "G2.2.1", "gr:3:2", "G0.3.0",
-    "G0.3.1", "lnb:1", "G0.0.1", "G1.3.0", "G1.3.1", "kg:0", "G3.2.0", "kg:1", "kg:2", "G1.0.0",
-    "G3.2.1", "kg:3", "G3.1.1", "G3.1.0", "kg:4", "kg:5", "G2.3.0", "branch", "G1.0.1", "G2.3.1",
-    "bout", "G3.3.0", "small", "G2.0.0", "convb:0", "S0", "G3.3.1", "G2.0.1", "S1", "convb:1",
-    "A0.0", "S2", "A0.1", "S3", "A1.0", "A1.1", "convb:2", "convb:3", "convb:4", "convb:5", "A2.0",
-    "A2.1",
+    "taps", "pix", "conv:0", "conv:1", "W1.1.0", "conv:2", "conv:3", "W1.1.1", "W1.2.0", "conv:4",
+    "W2.1.0", "conv:5", "W2.1.1", "W1.2.1", "cot", "ln", "h:0:0", "h:0:1", "W1.3.0", "h:0:2",
+    "W3.1.0", "W2.2.0", "h:0:3", "W3.1.1", "W1.3.1", "W2.2.1", "h:1:0", "h:1:1", "h:1:2", "h:1:3",
+    "gr:1:0", "gr:1:1", "gr:1:2", "G0.1.1", "gr:0:0", "W3.2.0", "W2.3.0", "gr:0:1", "G1.1.1",
+    "W3.2.1", "W2.3.1", "h:2:0", "G0.1.0", "h:2:1", "h:2:2", "h:2:3", "gr:2:0", "gr:2:1", "gr:2:2",
+    "G0.2.0", "gr:0:2", "G0.2.1", "W3.3.0", "G1.2.0", "W3.3.1", "G1.2.1", "G1.1.0", "h:3:0",
+    "h:3:1", "h:3:2", "h:3:3", "gr:3:0", "gr:3:1", "gr:3:2", "G2.2.0", "G0.0.1", "G0.3.1",
+    "G0.3.0", "G2.2.1", "ncot", "G1.3.1", "G3.2.0", "G1.3.0", "G1.0.1", "G3.2.1", "lnb", "kg:0",
+    "kg:1", "G0.0.0", "kg:2", "G2.3.1", "kg:3", "kg:4", "G1.0.0", "kg:5", "G2.3.0", "G3.3.1",
+    "branch", "bout", "G2.0.1", "G3.3.0", "G2.0.0", "small", "convb:0", "A0.1", "S0", "A0.0", "S1",
+    "A1.1", "A1.0", "convb:1", "convb:2", "convb:3", "S2", "convb:4", "convb:5", "A2.1", "S3",
+    "A2.0",
 )
 
 
@@ -59,22 +58,30 @@
     n_dp,
     n_tensor,
     pix_hbm,
-    side_ref,
+    side_hbm,
     cot_hbm,
-    taps_ref,
-    depth_bias_ref,
-    gain_ref,
-    shift_ref,
+    taps_hbm,
+    depth_bias_hbm,
+    gain_hbm,
+    shift_hbm,
     we_hbm,
-    eb_ref,
+    eb_hbm,
     wr_hbm,
-    rb_ref,
-    scale_ref,
+    rb_hbm,
+    scale_hbm,
     out_hbm,
     in_grad_hbm,
     gr_hbm,
     ge_hbm,
     small_hbm,
+    side_ref,
+    taps_ref,
+    depth_bias_ref,
+    gain_ref,
+    shift_ref,
+    eb_ref,
+    rb_ref,
+    scale_ref,
     stage,
     X,
     XH,
@@ -96,6 +103,7 @@
     R0,
     R1,
     R2,
+    RP,
     RZ,
     RX,
     OUTB,
@@ -166,7 +174,13 @@
         pltpu.make_async_copy(we_hbm, WE.at[0], load_sem.at[2]),
         pltpu.make_async_copy(wr_hbm, WR.at[0], load_sem.at[3]),
     ]
-    for copy in loads:
+    rows_in = [
+        (eb_hbm, eb_ref), (depth_bias_hbm, depth_bias_ref), (gain_hbm, gain_ref),
+        (shift_hbm, shift_ref), (rb_hbm, rb_ref), (scale_hbm, scale_ref), (side_hbm, side_ref),
+        (taps_hbm, taps_ref),
+    ]
+    rows_in = [pltpu.make_async_copy(a, b, load_sem.at[4 + i]) for i, (a, b) in enumerate(rows_in)]
+    for copy in rows_in + loads:
         copy.start()
 
     def vector(ref):
@@ -237,8 +251,12 @@
         if level < 4:
             w_copy(s, m, level).start()
 
+    pl.semaphore_wait(barrier, len(peers))
+    for m in range(2):
+        w_step(0, 0, m)
+    for copy in rows_in:
+        copy.wait()
     EB[tz] = jnp.broadcast_to(vector(eb_ref), (8, D))
-    pl.semaphore_wait(barrier, len(peers))
     for o in range(1, n_tensor):
         e_copy(o).start()
 
@@ -255,78 +273,101 @@
             start = start + g_second[m] * PIECE
         return start
 
+    PLANE = {0: 0, 2: 1, 3: 2}
+
     def g_copy(s, m, level):
         if level == 0:
-            start, size, peer, dst = (1 - core) * HALF, HALF, flip(0), R0
+            start, size, peer, dst = (1 - core) * HALF, HALF, flip(0), R0.at[s, m]
         elif level == 1:
             start = g_start(m, 0) + (1 - g_first[m]) * QUART
-            size, peer, dst = QUART, g_first_peer[m], R1
+            size, peer, dst = QUART, g_first_peer[m], R1.at[PLANE[s], m]
         else:
             start = g_start(m, 1) + (1 - g_second[m]) * PIECE
-            size, peer, dst = PIECE, g_second_peer[m], R2
+            size, peer, dst = PIECE, g_second_peer[m], R2.at[PLANE[s], m]
         src = GS.at[s, m, pl.ds(pl.multiple_of(start, 16), size), :]
-        return remote(
-            src, dst.at[s, m], g_send.at[s, m, level], g_recv.at[s, m, level], (peer, tz)
-        )
+        return remote(src, dst, g_send.at[s, m, level], g_recv.at[s, m, level], (peer, tz))
+
+    def p_copy(m):
+        src = GS.at[1, m, pl.ds(pl.multiple_of(core * HALF, 16), HALF), :]
+        return remote(src, RP.at[m], g_send.at[1, m, 1], g_recv.at[1, m, 1], (dp, partner))
 
     def z_copy(s, m):
         src = GS.at[s, m, pl.ds(pl.multiple_of(g_start(m, 2), 16), PIECE), :]
-        slot = 1 if s == 1 else 3 - middle
+        slot = 3 - middle
         return remote(
-            src, RZ.at[slot - 1, m], g_send.at[s, m, 3], g_recv.at[slot, m, 3], (dp, shard_of(s))
+            src, RZ.at[slot - 2, m], g_send.at[s, m, 3], g_recv.at[slot, m, 3], (dp, shard_of(s))
         )
 
     def z_arrival(s, m):
         src = GS.at[s, m, pl.ds(pl.multiple_of(g_start(m, 2), 16), PIECE), :]
-        return remote(src, RZ.at[s - 1, m], g_send.at[s, m, 3], g_recv.at[s, m, 3], (dp, partner))
+        return remote(src, RZ.at[s - 2, m], g_send.at[s, m, 3], g_recv.at[s, m, 3], (dp, partner))
 
     def g_step(level, s, m):
         if level > 0:
             g_copy(s, m, level - 1).wait_recv()
-            got = (R0, R1, R2)[level - 1]
+            got = [(R0.at[s, m], R1.at[PLANE.get(s, 0), m], R2.at[PLANE.get(s, 0), m])[level - 1]]
+            if s == 0 and level == 1:
+                p_copy(m).wait_recv()
+                got.append(RP.at[m])
             start = g_start(m, level - 1)
             size = (HALF, QUART, PIECE)[level - 1]
 
             def add(i, c):
                 rows = pl.ds(pl.multiple_of(start + i * 16, 16), 16)
-                GS[s, m, rows, :] = (
-                    GS[s, m, rows, :] + got[s, m, pl.ds(pl.multiple_of(i * 16, 16), 16), :]
-                )
+                mine = pl.ds(pl.multiple_of(i * 16, 16), 16)
+                total = GS[s, m, rows, :].astype(f32)
+                for ref in got:
+                    total = total + ref[mine, :].astype(f32)
+                GS[s, m, rows, :] = total.astype(bf16)
                 return c
 
             lax.fori_loop(0, size // 16, add, 0, unroll=2)
-        if level < 3:
+        if s == 1 and level == 1:
+            p_copy(m).start()
+        elif level < 3:
             g_copy(s, m, level).start()
         elif s > 0:
             z_copy(s, m).start()
 
+    def o_rows(m, level):
+        start = 0
+        if level <= 1:
+            start = start + g_first[m] * QUART
+        if level == 0:
+            start = start + g_second[m] * PIECE
+        return pl.ds(pl.multiple_of(start, 16), (PIECE, QUART, HALF)[level])
+
+    core_half = pl.ds(pl.multiple_of(core * HALF, 16), HALF)
+
     def a_copy(m, level):
-        if level == 0:
-            start, size, peer = g_start(m, 2), PIECE, g_second_peer[m]
-        elif level == 1:
-            start, size, peer = g_start(m, 1), QUART, g_first_peer[m]
-        else:
-            start, size, peer = g_start(m, 0), HALF, flip(0)
-        here = OUTB.at[m, pl.ds(pl.multiple_of(start, 16), size), :]
-        return remote(here, here, g_send.at[0, m, 3 + level], g_recv.at[0, m, 3 + level], (peer, tz))
+        here = OUTB.at[m, o_rows(m, level), :]
+        there = here if level < 2 else (gr_hbm, ge_hbm)[m].at[core_half, :]
+        peer = (g_second_peer[m], g_first_peer[m], flip(0))[level]
+        return remote(here, there, g_send.at[0, m, 3 + level], g_recv.at[0, m, 3 + level], (peer, tz))
+
+    def own_half(m):
+        return pltpu.make_async_copy(
+            OUTB.at[m], (gr_hbm, ge_hbm)[m].at[core_half, :], load_sem.at[m]
+        )
 
     def x_copy(m, b):
-        here = OUTB.at[m, pl.ds(pl.multiple_of(g_start(m, 2), 16), PIECE), :]
+        here = OUTB.at[m, o_rows(m, 0), :]
         return remote(here, RX.at[b - 3, m], x_send.at[b - 3, m], x_recv.at[b - 3, m], (flip(b), tz))
 
     def finish_sum(m):
         g_step(3, 0, m)
-        for s in range(1, SLOTS):
+        for s in range(2, SLOTS):
             z_arrival(s, m).wait_recv()
         start = g_start(m, 2)
+        there = start - core * HALF
 
         def add(i, c):
             rows = pl.ds(pl.multiple_of(start + i * 16, 16), 16)
             own = pl.ds(pl.multiple_of(i * 16, 16), 16)
             total = GS[0, m, rows, :].astype(f32)
-            for s in range(1, SLOTS):
-                total = total + RZ[s - 1, m, own, :].astype(f32)
-            OUTB[m, rows, :] = total.astype(bf16)
+            for s in range(2, SLOTS):
+                total = total + RZ[s - 2, m, own, :].astype(f32)
+            OUTB[m, pl.ds(pl.multiple_of(there + i * 16, 16), 16), :] = total.astype(bf16)
             return c
 
         lax.fori_loop(0, PIECE // 16, add, 0)
@@ -335,7 +376,7 @@
             x_copy(m, b).wait()
 
             def add_x(i, c):
-                rows = pl.ds(pl.multiple_of(start + i * 16, 16), 16)
+                rows = pl.ds(pl.multiple_of(there + i * 16, 16), 16)
                 OUTB[m, rows, :] = (
                     OUTB[m, rows, :] + RX[b - 3, m, pl.ds(pl.multiple_of(i * 16, 16), 16), :]
                 )
@@ -350,6 +391,8 @@
             a_copy(m, level - 1).wait_recv()
         if level < 3:
             a_copy(m, level).start()
+        if level == 2:
+            own_half(m).start()
 
     def sr_copy(j):
         dst_low = flip_low(j)
@@ -490,55 +533,62 @@
 
         lax.fori_loop(0, G, one, 0)
 
-    def layernorm(lo, hi):
+    def tree(parts):
+        parts = list(parts)
+        while len(parts) > 1:
+            parts = [
+                parts[i] + parts[i + 1] if i + 1 < len(parts) else parts[i]
+                for i in range(0, len(parts), 2)
+            ]
+        return parts[0]
+
+    def fold(v):
+        return tree(v[i : i + 8] for i in range(0, v.shape[0], 8))
+
+    def layernorm():
         gain = vector(gain_ref)
         shift = vector(shift_ref)
 
         def body(q, c):
-            rows = pl.ds(pl.multiple_of(q * 16, 16), 16)
+            rows = pl.ds(pl.multiple_of(q * 32, 32), 32)
             v = [XH[g, rows, :] for g in range(G)]
-            total = functools.reduce(jnp.add, v)
-            mean = jnp.sum(total, axis=1, keepdims=True) * (1.0 / D)
+            mean = jnp.sum(tree(v), axis=1, keepdims=True) * (1.0 / D)
             v = [a - mean for a in v]
-            total = functools.reduce(jnp.add, [a * a for a in v])
+            total = tree([a * a for a in v])
             rstd = lax.rsqrt(jnp.sum(total, axis=1, keepdims=True) * (1.0 / D) + norm_eps)
-            RSTD[rows, :] = jnp.broadcast_to(rstd, (16, LANES))
+            RSTD[rows, :] = jnp.broadcast_to(rstd, (32, LANES))
             for g in range(G):
                 xh = v[g] * rstd
                 XH[g, rows, :] = xh
                 NM[rows, lanes(g)] = (xh * gain[:, lanes(g)] + shift[:, lanes(g)]).astype(bf16)
             return c
 
-        lax.fori_loop(lo, hi, body, 0, unroll=5)
-
-    def layernorm_back(lo, hi):
+        lax.fori_loop(0, ROWS // 32, body, 0, unroll=5)
+
+    def layernorm_back():
         gain = vector(gain_ref)
 
         def body(q, sums):
-            gains, shifts, biases = [list(part) for part in sums]
-            rows = pl.ds(pl.multiple_of(q * 16, 16), 16)
+            rows = pl.ds(pl.multiple_of(q * 160, 32), 160)
             rstd = RSTD[rows, :]
             xh = [XH[g, rows, :] for g in range(G)]
             nc = [NC[g, rows, :] for g in range(G)]
             d = [nc[g] * gain[:, lanes(g)] for g in range(G)]
-            s1 = functools.reduce(jnp.add, d)
-            s2 = functools.reduce(jnp.add, [d[g] * xh[g] for g in range(G)])
-            m1 = jnp.sum(s1, axis=1, keepdims=True) * (1.0 / D)
-            m2 = jnp.sum(s2, axis=1, keepdims=True) * (1.0 / D)
+            m1 = jnp.sum(tree(d), axis=1, keepdims=True) * (1.0 / D)
+            m2 = jnp.sum(tree([a * b for a, b in zip(d, xh)]), axis=1, keepdims=True) * (1.0 / D)
+            out = []
             for g in range(G):
                 dm = rstd * (d[g] - m1 - xh[g] * m2)
                 NC[g, rows, :] = dm
-                gx = nc[g] * xh[g]
-                gains[g] = gains[g] + (gx[:8] + gx[8:])
-                shifts[g] = shifts[g] + (nc[g][:8] + nc[g][8:])
-                biases[g] = biases[g] + (dm[:8] + dm[8:])
-            return tuple(gains), tuple(shifts), tuple(biases)
-
-        zeros = (jnp.zeros((8, LANES), f32),) * G
-        sums = lax.fori_loop(lo, hi, body, (zeros, zeros, zeros), unroll=5)
+                old = sums[g]
+                out.append((old[0] + fold(nc[g] * xh[g]), old[1] + fold(nc[g]), old[2] + fold(dm)))
+            return tuple(out)
+
+        zero = jnp.zeros((8, LANES), f32)
+        sums = lax.fori_loop(0, ROWS // 160, body, ((zero, zero, zero),) * G)
         for i in range(3):
             for g in range(G):
-                ACC[i, g] = sums[i][g] if lo == 0 else ACC[i, g] + sums[i][g]
+                ACC[i, g] = sums[g][i]
 
     def kernel_grad(between):
         def one(g, carry):
@@ -742,12 +792,6 @@
         where = [int(v) for v in rest.split(":")] if rest else []
         if "." in name or kind[0] == "S":
             tell(name)
-        elif kind == "ln":
-            n = ROWS // 16
-            layernorm(n * where[0] // 20 * 5, n * (where[0] + 1) // 20 * 5)
-        elif kind == "lnb":
-            n = ROWS // 16
-            layernorm_back(n * where[0] // 2, n * (where[0] + 1) // 2)
         elif kind == "h":
             if where[1] == 0:
                 linears_ready(where[0])
@@ -759,6 +803,8 @@
                 "pix": pixels_in,
                 "taps": load_taps,
                 "cot": cot_in,
+                "ln": layernorm,
+                "lnb": layernorm_back,
                 "ncot": back_to_normed,
                 "branch": to_branch,
                 "bout": start_output,
@@ -775,15 +821,13 @@
         else:
             step(PLAN[at])
             at += 1
-    for m in range(2):
-        a_step(3, m)
     tail = [
-        pltpu.make_async_copy(OUTB.at[0], gr_hbm, load_sem.at[0]),
-        pltpu.make_async_copy(OUTB.at[1], ge_hbm, load_sem.at[1]),
         pltpu.make_async_copy(SALL, small_hbm, load_sem.at[2]),
     ]
     for copy in tail:
         copy.start()
+    for m in range(2):
+        a_step(3, m)
     for m in range(2):
         own_pieces(m)[0].wait_send()
         in_middle(own_pieces(m)[1].wait_send)
@@ -793,12 +837,14 @@
             in_middle(relay(s, m).wait_send)
             for level in range(1, 4):
                 w_copy(s, m, level).wait_send()
-            z_copy(s, m).wait_send()
+            if s > 1:
+                z_copy(s, m).wait_send()
     for s in range(SLOTS):
         for m in range(2):
-            for level in range(3):
+            for level in range(3 if s != 1 else 1):
                 g_copy(s, m, level).wait_send()
     for m in range(2):
+        p_copy(m).wait_send()
         for level in range(3):
             a_copy(m, level).wait_send()
     for j in range(1, 8):
@@ -811,20 +857,26 @@
         out_copy(g).wait()
     for copy in tail:
         copy.wait()
+    for m in range(2):
+        own_half(m).wait()
 
 
 def hand_over(
     out_in, grad_in, gr, ge, small,
     block_out, input_grad, kernel_grad, bias_grad, gain_grad, shift_grad,
     expand_grad, expand_bias_grad, reduce_grad, reduce_bias_grad, scale_grad,
-    narrow, wide, whole_sem, in_sem, out_sem,
+    narrow, wide, grad_rows, out_rows, there_sem, back_sem, in_sem, out_sem,
 ):
     D = gr.shape[0]
     third = D // 3
-    whole = [
-        pltpu.make_async_copy(grad_in, input_grad, whole_sem.at[0]),
-        pltpu.make_async_copy(out_in, block_out, whole_sem.at[1]),
+    half = out_in.shape[0] // 2
+    halves = [
+        (held.at[pl.ds(i * half, half)], src.at[pl.ds(i * half, half)], dst.at[pl.ds(i * half, half)])
+        for i in range(2)
+        for held, src, dst in ((grad_rows, grad_in, input_grad), (out_rows, out_in, block_out))
     ]
+    there = [pltpu.make_async_copy(v[1], v[0], there_sem.at[i]) for i, v in enumerate(halves)]
+    back = [pltpu.make_async_copy(v[0], v[2], back_sem.at[i]) for i, v in enumerate(halves)]
     parts = [(i, m) for i in range(3) for m in range(2)]
 
     def rows(i):
@@ -842,8 +894,6 @@
     }
     for part in parts:
         reads[part].start()
-    for copy in whole:
-        copy.start()
     kernel_grad[...] = small[:TAPS, :]
     own = ROW_EXPAND + lax.axis_index("tensor")
     for row, ref in (
@@ -854,6 +904,9 @@
     expand_bias_grad[...] = small[pl.ds(own, 1), :].reshape(D)
     for i, m in parts:
         reads[i, m].wait()
+        if i == 0 and m == 0:
+            for copy in there:
+                copy.start()
 
         def widen(k, c):
             at = pl.ds(pl.multiple_of(i * third + k * 32, 32), 32)
@@ -862,9 +915,12 @@
 
         lax.fori_loop(0, third // 32, widen, 0)
         writes[i, m].start()
+    for arrived, copy in zip(there, back):
+        arrived.wait()
+        copy.start()
     for part in parts:
         writes[part].wait()
-    for copy in whole:
+    for copy in back:
         copy.wait()
 
 
@@ -891,10 +947,9 @@
     extra = max(n_dp.bit_length() - 4, 1)
     vmem = pl.BlockSpec(memory_space=pltpu.VMEM)
     hbm = pl.BlockSpec(memory_space=pltpu.HBM)
-    smem = pl.BlockSpec(memory_space=pltpu.SMEM)
     V = pltpu.VMEM
     DMA = pltpu.SemaphoreType.DMA
-    scratch = [
+    scratch = [pltpu.SMEM((img,), jnp.int32), V((TAPS, D), bf16)] + [V((D,), bf16) for _ in range(6)] + [
         V((8, rows, LANES), f32),
         V((G, rows, LANES), f32),
         V((G, rows, LANES), f32),
@@ -914,17 +969,18 @@
         V((5, G, 8, LANES), f32),
         V((slots, 2, D, D), bf16),
         V((slots, 2, D // 2, D), bf16),
-        V((slots, 2, D // 4, D), bf16),
-        V((slots, 2, D // 8, D), bf16),
+        V((slots - 1, 2, D // 4, D), bf16),
         V((slots - 1, 2, D // 8, D), bf16),
+        V((2, D // 2, D), bf16),
+        V((slots - 2, 2, D // 8, D), bf16),
         V((extra, 2, D // 8 if n_dp > 8 else 16, D), bf16),
-        V((2, D, D), bf16),
+        V((2, D // 2, D), bf16),
         V((SMALL, D), f32),
         V((7, 8, D), f32),
         V((slots, 8, D), f32),
         V((extra, 8, D), f32),
         V((SMALL, D), f32),
-        DMA((4,)),
+        DMA((12,)),
         DMA((1 + G,)),
         DMA((slots, 2, 4)),
         DMA((slots, 2, 4)),
@@ -946,11 +1002,11 @@
             jax.ShapeDtypeStruct((D, D), bf16),
             jax.ShapeDtypeStruct((SMALL, D), f32),
         ],
-        in_specs=[hbm, smem, hbm, vmem, vmem, vmem, vmem, hbm, vmem, hbm, vmem, vmem],
+        in_specs=[hbm] * 12,
         out_specs=[hbm] * 5,
         scratch_shapes=scratch,
         compiler_params=pltpu.CompilerParams(
-            collective_id=0, has_side_effects=True, vmem_limit_bytes=61 << 20
+            collective_id=0, has_side_effects=True, vmem_limit_bytes=63 << 20
         ),
         cost_estimate=pl.CostEstimate(
             flops=12 * rows * D * D * slots, bytes_accessed=20 * rows * D, transcendentals=0
@@ -984,7 +1040,10 @@
         scratch_shapes=[
             V((2, D, D), bf16),
             V((2, D, D), f32),
-            DMA((2,)),
+            V((rows, D), f32),
+            V((rows, D), bf16),
+            DMA((4,)),
+            DMA((4,)),
             DMA((2, 3)),
             DMA((2, 3)),
         ],

time: 237 us -> 120 us (0.51)
  Pallas kernels: 236 us -> 119 us
    pallas_call x1, Pallas kernels: 115 us -> 8.07 us  [per_device(): pl.pallas_call(hand_over, out_shape=[jax.ShapeDtypeStruct((rows, D), bf16...]
    pallas_call x1, Pallas kernels: 121 us -> 111 us  [per_device(): pl.pallas_call(functools.partial(kernel, n_dp, n_tensor), out_shape=[jax....]
where the time goes in v3:
time: 120 us
  Pallas kernels  119 us (99%)
    pallas_call x1, Pallas kernels, per_device(): pl.pallas_call(functools.partial(kernel, n_dp, n_tensor), out_shape=[jax....  111 us
    pallas_call x1, Pallas kernels, per_device(): pl.pallas_call(hand_over, out_shape=[jax.ShapeDtypeStruct((rows, D), bf16...  8.07 us

profile of v3, /device:TPU:0, one launch (start us, length us, event | category | flops | bytes accessed | tf_op | source)
XLA Modules:
  0.0 119.9 jit_solution(10239553903972413556)
XLA Ops:
  0.6 111.0 %shard_map.203 = (bf16[800,768]{1,0:T(8,128)(2,1)}, f32[800,768]{1,0:T(8,128)}, bf16[768,768]{1,0:T(8,128)(2,1)}, bf16[768,768]{1,0:T(8,128)(2,1)}, f32[64,768]{1,0:T(8,128)}) custom-call(bf16[800,768]{1,0:T(8,128)(2,1)} %pix_hbm.1, s32[8]{0:T(128)} %side_hbm.1, bf16[800,768]{1,0:T(8,128)(2,1)} %cot_hbm.1, bf16[49,768]{1,0:T(8,128)(2,1)} %taps_hbm.1, ...), custom_call_target="tpu_custom_call" | custom-call | flops 22649241600 | bytes 12288000 | tf_op jit(solution)/shard_map/pallas_call | solution.py:996
  111.7 8.1 %shard_map.204 = (bf16[800,768]{1,0:T(8,128)(2,1)}, f32[800,768]{1,0:T(8,128)}, f32[49,768]{1,0:T(8,128)}, f32[768]{0:T(1024)}, f32[768]{0:T(1024)}, /*index=5*/...) custom-call(bf16[800,768]{1,0:T(8,128)(2,1)} %get-tuple-element.16.o, ...), custom_call_target="tpu_custom_call" | custom-call | tf_op jit(solution)/shard_map/pallas_call | solution.py:1030

commit v4 on v3

--- a/solution.py
+++ b/solution.py
@@ -21,18 +21,17 @@
 ROW_BIAS, ROW_GAIN, ROW_SHIFT, ROW_REDUCE, ROW_SCALE, ROW_EXPAND = 49, 50, 51, 52, 53, 54
 SMALL = 64
 PLAN = (
-    "taps", "pix", "conv:0", "conv:1", "W1.1.0", "conv:2", "conv:3", "W1.1.1", "W1.2.0", "conv:4",
-    "W2.1.0", "conv:5", "W2.1.1", "W1.2.1", "cot", "ln", "h:0:0", "h:0:1", "W1.3.0", "h:0:2",
-    "W3.1.0", "W2.2.0", "h:0:3", "W3.1.1", "W1.3.1", "W2.2.1", "h:1:0", "h:1:1", "h:1:2", "h:1:3",
-    "gr:1:0", "gr:1:1", "gr:1:2", "G0.1.1", "gr:0:0", "W3.2.0", "W2.3.0", "gr:0:1", "G1.1.1",
-    "W3.2.1", "W2.3.1", "h:2:0", "G0.1.0", "h:2:1", "h:2:2", "h:2:3", "gr:2:0", "gr:2:1", "gr:2:2",
-    "G0.2.0", "gr:0:2", "G0.2.1", "W3.3.0", "G1.2.0", "W3.3.1", "G1.2.1", "G1.1.0", "h:3:0",
-    "h:3:1", "h:3:2", "h:3:3", "gr:3:0", "gr:3:1", "gr:3:2", "G2.2.0", "G0.0.1", "G0.3.1",
-    "G0.3.0", "G2.2.1", "ncot", "G1.3.1", "G3.2.0", "G1.3.0", "G1.0.1", "G3.2.1", "lnb", "kg:0",
-    "kg:1", "G0.0.0", "kg:2", "G2.3.1", "kg:3", "kg:4", "G1.0.0", "kg:5", "G2.3.0", "G3.3.1",
-    "branch", "bout", "G2.0.1", "G3.3.0", "G2.0.0", "small", "convb:0", "A0.1", "S0", "A0.0", "S1",
-    "A1.1", "A1.0", "convb:1", "convb:2", "convb:3", "S2", "convb:4", "convb:5", "A2.1", "S3",
-    "A2.0",
+    "taps", "pix", "conv:0", "conv:1", "W1.1.0", "W1.2.0", "conv:2", "W1.1.1", "conv:3", "W2.1.0",
+    "W1.2.1", "conv:4", "W2.1.1", "conv:5", "cot", "W3.1.0", "W1.3.0", "ln", "W2.2.1", "h:0:0",
+    "h:0:1", "W2.2.0", "W1.3.1", "W3.1.1", "h:0:2", "h:0:3", "h:1:0", "h:1:1", "h:1:2", "h:1:3",
+    "gr:1:0", "G0.1.0", "W2.3.0", "W3.2.1", "gr:1:1", "W3.2.0", "G1.1.0", "W2.3.1", "gr:0:0",
+    "h:2:0", "h:2:1", "W3.3.0", "h:2:2", "G0.1.1", "h:2:3", "gr:2:1", "W3.3.1", "gr:2:0", "G1.1.1",
+    "G0.2.0", "h:3:0", "h:3:1", "G0.2.1", "G1.2.0", "h:3:2", "h:3:3", "gr:3:0", "G1.2.1", "ncot",
+    "G0.3.0", "G2.2.0", "G0.0.0", "gr:3:1", "G2.2.1", "gr:0:1", "G0.3.1", "G1.3.0", "lnb",
+    "G1.0.0", "G3.2.1", "G3.2.0", "branch", "G2.3.0", "bout", "G0.0.1", "G2.0.0", "G1.3.1", "kg:0",
+    "G3.3.0", "G1.0.1", "kg:1", "kg:2", "kg:3", "G2.3.1", "kg:4", "kg:5", "A0.0", "small", "S0",
+    "G2.0.1", "G3.3.1", "convb:0", "A1.0", "convb:1", "S1", "A0.1", "convb:2", "convb:3", "A1.1",
+    "S2", "convb:4", "A2.0", "convb:5", "S3", "A2.1",
 )
 
 
@@ -129,7 +128,7 @@
     G = D // LANES
     ROWS = NM.shape[0]
     IMG = ROWS // PLACES
-    HALF, QUART, PIECE = D // 2, D // 4, D // 8
+    HALF, QUART, PIECE, BIT = D // 2, D // 4, D // 8, D // 16
     SLOTS = n_tensor
     extra = n_dp.bit_length() - 4
     dp = lax.axis_index("dp")
@@ -192,37 +191,39 @@
             device_id=device, device_id_type=MESH,
         )
 
-    W = (WE, WR)
+    PARTS = (0, 1)
     first = (xb, yb)
     second = (yb, xb)
     first_peer = (flip(1), flip(2))
     second_peer = (flip(2), flip(1))
-
-    def w_rows(m, level):
-        start = core * HALF
-        if level <= 2:
-            start = start + second[m] * QUART
+    W = (WE, WR)
+    core_half = pl.ds(pl.multiple_of(core * HALF, 16), HALF)
+
+    def w_rows(h, level):
+        start = core * HALF + h * QUART + second[h] * PIECE
         if level <= 1:
-            start = start + first[m] * PIECE
-        size = (PIECE, PIECE, QUART, HALF)[level]
-        return pl.ds(pl.multiple_of(start, 16), size)
-
-    def w_copy(s, m, level):
-        here = W[m].at[s, w_rows(m, level), :]
-        device = ((first_peer[m], tz), (second_peer[m], tz), (flip(0), tz))[level - 1]
-        return remote(here, here, w_send.at[s, m, level], w_recv.at[s, m, level], device)
-
-    def z_piece(m, source, slot, device):
-        rows = w_rows(m, 0)
+            start = start + first[h] * BIT
+        return pl.ds(pl.multiple_of(start, 16), (BIT, BIT, PIECE)[level])
+
+    def w_copy(s, m, level, h=0):
+        if level == 3:
+            here, device, i = W[m].at[s, core_half, :], flip(0), 6
+        else:
+            here = W[m].at[s, w_rows(h, level), :]
+            device, i = (first_peer[h], second_peer[h])[level - 1], 2 * level + h
+        return remote(here, here, w_send.at[s, m, i], w_recv.at[s, m, i], (device, tz))
+
+    def z_piece(m, h, source, slot, device):
+        rows = w_rows(h, 0)
         src = (we_hbm, wr_hbm)[m].at[rows, :] if source == 0 else W[m].at[source, rows, :]
-        send = w_send.at[0, m, slot] if source == 0 else w_send.at[source, m, 0]
-        return remote(src, W[m].at[slot, rows, :], send, w_recv.at[slot, m, 0], (dp, device))
-
-    def own_pieces(m):
-        return z_piece(m, 0, 1, partner), z_piece(m, 0, 2, across)
-
-    def relay(s, m):
-        return z_piece(m, 1, 3, across) if s == 1 else z_piece(m, s, s, partner)
+        send = w_send.at[0, m, 2 * slot + h] if source == 0 else w_send.at[source, m, h]
+        return remote(src, W[m].at[slot, rows, :], send, w_recv.at[slot, m, h], (dp, device))
+
+    def own_pieces(m, h):
+        return z_piece(m, h, 0, 1, partner), z_piece(m, h, 0, 2, across)
+
+    def relay(s, m, h):
+        return z_piece(m, h, 1, 3, across) if s == 1 else z_piece(m, h, s, s, partner)
 
     def in_middle(act):
         @pl.when(middle == 1)
@@ -239,17 +240,25 @@
 
     def w_step(level, s, m):
         if level == 0:
-            to_partner, to_other = own_pieces(m)
-            to_partner.start()
-            in_middle(to_other.start)
-            return
-        if level == 1:
-            z_piece(m, 0, s, partner).wait_recv()
-            in_middle(relay(s, m).start)
+            for h in PARTS:
+                own_pieces(m, h)[0].start()
+            for h in PARTS:
+                in_middle(own_pieces(m, h)[1].start)
+        elif level == 1:
+            for h in PARTS:
+                z_piece(m, h, 0, s, partner).wait_recv()
+                w_copy(s, m, 1, h).start()
+                in_middle(relay(s, m, h).start)
+        elif level == 2:
+            for h in PARTS:
+                w_copy(s, m, 1, h).wait_recv()
+                w_copy(s, m, 2, h).start()
+        elif level == 3:
+            for h in PARTS:
+                w_copy(s, m, 2, h).wait_recv()
+            w_copy(s, m, 3).start()
         else:
-            w_copy(s, m, level - 1).wait_recv()
-        if level < 4:
-            w_copy(s, m, level).start()
+            w_copy(s, m, 3).wait_recv()
 
     pl.semaphore_wait(barrier, len(peers))
     for m in range(2):
@@ -260,105 +269,123 @@
     for o in range(1, n_tensor):
         e_copy(o).start()
 
-    g_first = (yb, xb)
-    g_second = (xb, yb)
-    g_first_peer = (flip(2), flip(1))
-    g_second_peer = (flip(1), flip(2))
-
-    def g_start(m, level):
-        start = core * HALF
+    def g_start(h, level):
+        start = core * HALF + h * QUART
         if level >= 1:
-            start = start + g_first[m] * QUART
+            start = start + first[h] * PIECE
         if level >= 2:
-            start = start + g_second[m] * PIECE
+            start = start + second[h] * BIT
         return start
 
     PLANE = {0: 0, 2: 1, 3: 2}
 
-    def g_copy(s, m, level):
+    def g_copy(s, m, level, h=0):
         if level == 0:
-            start, size, peer, dst = (1 - core) * HALF, HALF, flip(0), R0.at[s, m]
+            start, size, peer, dst, i = (1 - core) * HALF, HALF, flip(0), R0.at[s, m], 0
         elif level == 1:
-            start = g_start(m, 0) + (1 - g_first[m]) * QUART
-            size, peer, dst = QUART, g_first_peer[m], R1.at[PLANE[s], m]
+            start = g_start(h, 0) + (1 - first[h]) * PIECE
+            size, peer, dst, i = PIECE, first_peer[h], R1.at[PLANE[s], m, h], 1 + h
         else:
-            start = g_start(m, 1) + (1 - g_second[m]) * PIECE
-            size, peer, dst = PIECE, g_second_peer[m], R2.at[PLANE[s], m]
+            start = g_start(h, 1) + (1 - second[h]) * BIT
+            size, peer, dst, i = BIT, second_peer[h], R2.at[PLANE[s], m, h], 3 + h
         src = GS.at[s, m, pl.ds(pl.multiple_of(start, 16), size), :]
-        return remote(src, dst, g_send.at[s, m, level], g_recv.at[s, m, level], (peer, tz))
+        return remote(src, dst, g_send.at[s, m, i], g_recv.at[s, m, i], (peer, tz))
 
     def p_copy(m):
-        src = GS.at[1, m, pl.ds(pl.multiple_of(core * HALF, 16), HALF), :]
+        src = GS.at[1, m, core_half, :]
         return remote(src, RP.at[m], g_send.at[1, m, 1], g_recv.at[1, m, 1], (dp, partner))
 
-    def z_copy(s, m):
-        src = GS.at[s, m, pl.ds(pl.multiple_of(g_start(m, 2), 16), PIECE), :]
+    def z_copy(s, m, h):
+        src = GS.at[s, m, pl.ds(pl.multiple_of(g_start(h, 2), 16), BIT), :]
         slot = 3 - middle
         return remote(
-            src, RZ.at[slot - 2, m], g_send.at[s, m, 3], g_recv.at[slot, m, 3], (dp, shard_of(s))
+            src, RZ.at[slot - 2, m, h], g_send.at[s, m, 5 + h], g_recv.at[slot, m, 5 + h],
+            (dp, shard_of(s)),
         )
 
-    def z_arrival(s, m):
-        src = GS.at[s, m, pl.ds(pl.multiple_of(g_start(m, 2), 16), PIECE), :]
-        return remote(src, RZ.at[s - 2, m], g_send.at[s, m, 3], g_recv.at[s, m, 3], (dp, partner))
+    def z_arrival(s, m, h):
+        src = GS.at[s, m, pl.ds(pl.multiple_of(g_start(h, 2), 16), BIT), :]
+        return remote(
+            src, RZ.at[s - 2, m, h], g_send.at[s, m, 5 + h], g_recv.at[s, m, 5 + h], (dp, partner)
+        )
+
+    def add_rows(s, m, start, size, got):
+        def add(i, c):
+            rows = pl.ds(pl.multiple_of(start + i * 16, 16), 16)
+            mine = pl.ds(pl.multiple_of(i * 16, 16), 16)
+            total = GS[s, m, rows, :].astype(f32)
+            for ref in got:
+                total = total + ref[mine, :].astype(f32)
+            GS[s, m, rows, :] = total.astype(bf16)
+            return c
+
+        lax.fori_loop(0, size // 16, add, 0, unroll=3)
 
     def g_step(level, s, m):
-        if level > 0:
-            g_copy(s, m, level - 1).wait_recv()
-            got = [(R0.at[s, m], R1.at[PLANE.get(s, 0), m], R2.at[PLANE.get(s, 0), m])[level - 1]]
-            if s == 0 and level == 1:
+        if level == 0:
+            g_copy(s, m, 0).start()
+        elif level == 1:
+            g_copy(s, m, 0).wait_recv()
+            got = [R0.at[s, m]]
+            if s == 0:
                 p_copy(m).wait_recv()
                 got.append(RP.at[m])
-            start = g_start(m, level - 1)
-            size = (HALF, QUART, PIECE)[level - 1]
-
-            def add(i, c):
-                rows = pl.ds(pl.multiple_of(start + i * 16, 16), 16)
-                mine = pl.ds(pl.multiple_of(i * 16, 16), 16)
-                total = GS[s, m, rows, :].astype(f32)
-                for ref in got:
-                    total = total + ref[mine, :].astype(f32)
-                GS[s, m, rows, :] = total.astype(bf16)
-                return c
-
-            lax.fori_loop(0, size // 16, add, 0, unroll=2)
-        if s == 1 and level == 1:
-            p_copy(m).start()
-        elif level < 3:
-            g_copy(s, m, level).start()
-        elif s > 0:
-            z_copy(s, m).start()
-
-    def o_rows(m, level):
-        start = 0
-        if level <= 1:
-            start = start + g_first[m] * QUART
+            if s == 1:
+                add_rows(s, m, core * HALF, HALF, got)
+                p_copy(m).start()
+            else:
+                for h in PARTS:
+                    for side in range(2):
+                        bit = 1 - first[h] if side == 0 else first[h]
+                        at = h * QUART + bit * PIECE
+                        add_rows(
+                            s, m, core * HALF + at, PIECE,
+                            [ref.at[pl.ds(pl.multiple_of(at, 16), PIECE), :] for ref in got],
+                        )
+                        if side == 0:
+                            g_copy(s, m, 1, h).start()
+        elif level == 2:
+            for h in PARTS:
+                g_copy(s, m, 1, h).wait_recv()
+                add_rows(s, m, g_start(h, 1), PIECE, [R1.at[PLANE[s], m, h]])
+                g_copy(s, m, 2, h).start()
+        else:
+            for h in PARTS:
+                g_copy(s, m, 2, h).wait_recv()
+                add_rows(s, m, g_start(h, 2), BIT, [R2.at[PLANE[s], m, h]])
+                if s > 0:
+                    z_copy(s, m, h).start()
+
+    def o_rows(h, level):
+        start = h * QUART + first[h] * PIECE
         if level == 0:
-            start = start + g_second[m] * PIECE
-        return pl.ds(pl.multiple_of(start, 16), (PIECE, QUART, HALF)[level])
-
-    core_half = pl.ds(pl.multiple_of(core * HALF, 16), HALF)
-
-    def a_copy(m, level):
-        here = OUTB.at[m, o_rows(m, level), :]
-        there = here if level < 2 else (gr_hbm, ge_hbm)[m].at[core_half, :]
-        peer = (g_second_peer[m], g_first_peer[m], flip(0))[level]
-        return remote(here, there, g_send.at[0, m, 3 + level], g_recv.at[0, m, 3 + level], (peer, tz))
+            start = start + second[h] * BIT
+        return pl.ds(pl.multiple_of(start, 16), (BIT, PIECE)[level])
+
+    def a_copy(m, level, h=0):
+        if level == 2:
+            here, there = OUTB.at[m], (gr_hbm, ge_hbm)[m].at[core_half, :]
+            peer, i = flip(0), 11
+        else:
+            here = there = OUTB.at[m, o_rows(h, level), :]
+            peer, i = (second_peer[h], first_peer[h])[level], 7 + 2 * level + h
+        return remote(here, there, g_send.at[0, m, i], g_recv.at[0, m, i], (peer, tz))
 
     def own_half(m):
         return pltpu.make_async_copy(
             OUTB.at[m], (gr_hbm, ge_hbm)[m].at[core_half, :], load_sem.at[m]
         )
 
-    def x_copy(m, b):
-        here = OUTB.at[m, o_rows(m, 0), :]
-        return remote(here, RX.at[b - 3, m], x_send.at[b - 3, m], x_recv.at[b - 3, m], (flip(b), tz))
-
-    def finish_sum(m):
-        g_step(3, 0, m)
+    def x_copy(m, b, h):
+        here = OUTB.at[m, o_rows(h, 0), :]
+        return remote(
+            here, RX.at[b - 3, m, h], x_send.at[b - 3, m, h], x_recv.at[b - 3, m, h], (flip(b), tz)
+        )
+
+    def finish_sum(m, h):
         for s in range(2, SLOTS):
-            z_arrival(s, m).wait_recv()
-        start = g_start(m, 2)
+            z_arrival(s, m, h).wait_recv()
+        start = g_start(h, 2)
         there = start - core * HALF
 
         def add(i, c):
@@ -366,33 +393,41 @@
             own = pl.ds(pl.multiple_of(i * 16, 16), 16)
             total = GS[0, m, rows, :].astype(f32)
             for s in range(2, SLOTS):
-                total = total + RZ[s - 2, m, own, :].astype(f32)
+                total = total + RZ[s - 2, m, h, own, :].astype(f32)
             OUTB[m, pl.ds(pl.multiple_of(there + i * 16, 16), 16), :] = total.astype(bf16)
             return c
 
-        lax.fori_loop(0, PIECE // 16, add, 0)
+        lax.fori_loop(0, BIT // 16, add, 0)
         for b in range(3, 3 + extra):
-            x_copy(m, b).start()
-            x_copy(m, b).wait()
+            x_copy(m, b, h).start()
+            x_copy(m, b, h).wait()
 
             def add_x(i, c):
                 rows = pl.ds(pl.multiple_of(there + i * 16, 16), 16)
                 OUTB[m, rows, :] = (
-                    OUTB[m, rows, :] + RX[b - 3, m, pl.ds(pl.multiple_of(i * 16, 16), 16), :]
+                    OUTB[m, rows, :] + RX[b - 3, m, h, pl.ds(pl.multiple_of(i * 16, 16), 16), :]
                 )
                 return c
 
-            lax.fori_loop(0, PIECE // 16, add_x, 0)
+            lax.fori_loop(0, BIT // 16, add_x, 0)
 
     def a_step(level, m):
         if level == 0:
-            finish_sum(m)
+            g_step(3, 0, m)
+            for h in PARTS:
+                finish_sum(m, h)
+                a_copy(m, 0, h).start()
+        elif level == 1:
+            for h in PARTS:
+                a_copy(m, 0, h).wait_recv()
+                a_copy(m, 1, h).start()
+        elif level == 2:
+            for h in PARTS:
+                a_copy(m, 1, h).wait_recv()
+            a_copy(m, 2).start()
+            own_half(m).start()
         else:
-            a_copy(m, level - 1).wait_recv()
-        if level < 3:
-            a_copy(m, level).start()
-        if level == 2:
-            own_half(m).start()
+            a_copy(m, 2).wait_recv()
 
     def sr_copy(j):
         dst_low = flip_low(j)
@@ -643,10 +678,13 @@
                     total = w if total is None else total + w
                 EBG[s, :, mine] = total
 
-    def grad_block(s, j):
-        cols = slice(j * BLOCK, (j + 1) * BLOCK)
-        GS[s, 0, cols, :] = dot_rows(ACT[s, :, cols], BC[...]).astype(bf16)
-        GS[s, 1, :, cols] = dot_rows(NM[...], HC[s, :, cols]).astype(bf16)
+    def grad_block(s, m):
+        for j in range(D // BLOCK):
+            cols = slice(j * BLOCK, (j + 1) * BLOCK)
+            if m == 0:
+                GS[s, 0, cols, :] = dot_rows(ACT[s, :, cols], BC[...]).astype(bf16)
+            else:
+                GS[s, 1, :, cols] = dot_rows(NM[...], HC[s, :, cols]).astype(bf16)
 
     def back_to_normed():
         for n in range(D // BLOCK):
@@ -828,25 +866,29 @@
         copy.start()
     for m in range(2):
         a_step(3, m)
-    for m in range(2):
-        own_pieces(m)[0].wait_send()
-        in_middle(own_pieces(m)[1].wait_send)
     for s in range(1, SLOTS):
         e_copy(s).wait_send()
-        for m in range(2):
-            in_middle(relay(s, m).wait_send)
-            for level in range(1, 4):
-                w_copy(s, m, level).wait_send()
-            if s > 1:
-                z_copy(s, m).wait_send()
-    for s in range(SLOTS):
-        for m in range(2):
-            for level in range(3 if s != 1 else 1):
-                g_copy(s, m, level).wait_send()
     for m in range(2):
+        for h in PARTS:
+            own_pieces(m, h)[0].wait_send()
+            in_middle(own_pieces(m, h)[1].wait_send)
+            for s in range(1, SLOTS):
+                in_middle(relay(s, m, h).wait_send)
+                for level in (1, 2):
+                    w_copy(s, m, level, h).wait_send()
+            for s in PLANE:
+                for level in (1, 2):
+                    g_copy(s, m, level, h).wait_send()
+                if s > 0:
+                    z_copy(s, m, h).wait_send()
+            for level in range(2):
+                a_copy(m, level, h).wait_send()
+        for s in range(SLOTS):
+            if s > 0:
+                w_copy(s, m, 3).wait_send()
+            g_copy(s, m, 0).wait_send()
         p_copy(m).wait_send()
-        for level in range(3):
-            a_copy(m, level).wait_send()
+        a_copy(m, 2).wait_send()
     for j in range(1, 8):
         sr_copy(j).wait_send()
         sa_copy(j).wait_send()
@@ -865,8 +907,9 @@
     out_in, grad_in, gr, ge, small,
     block_out, input_grad, kernel_grad, bias_grad, gain_grad, shift_grad,
     expand_grad, expand_bias_grad, reduce_grad, reduce_bias_grad, scale_grad,
-    narrow, wide, grad_rows, out_rows, there_sem, back_sem, in_sem, out_sem,
+    narrow, wide, grad_rows, out_rows, sums, taps, *rest,
 ):
+    vectors, (there_sem, back_sem, in_sem, out_sem, small_sem) = rest[:6], rest[6:]
     D = gr.shape[0]
     third = D // 3
     half = out_in.shape[0] // 2
@@ -892,16 +935,20 @@
         )
         for i, m in parts
     }
+    load = pltpu.make_async_copy(small, sums, small_sem.at[0])
+    load.start()
     for part in parts:
         reads[part].start()
-    kernel_grad[...] = small[:TAPS, :]
+    load.wait()
+    taps[...] = sums[:TAPS, :]
     own = ROW_EXPAND + lax.axis_index("tensor")
-    for row, ref in (
+    given = [pltpu.make_async_copy(taps, kernel_grad, small_sem.at[0])]
+    for i, (row, ref) in enumerate((
         (ROW_BIAS, bias_grad), (ROW_GAIN, gain_grad), (ROW_SHIFT, shift_grad),
-        (ROW_REDUCE, reduce_bias_grad), (ROW_SCALE, scale_grad),
-    ):
-        ref[...] = small[row : row + 1, :].reshape(D)
-    expand_bias_grad[...] = small[pl.ds(own, 1), :].reshape(D)
+        (ROW_REDUCE, reduce_bias_grad), (ROW_SCALE, scale_grad), (own, expand_bias_grad),
+    )):
+        vectors[i][...] = sums[pl.ds(row, 1), :].reshape(D)
+        given.append(pltpu.make_async_copy(vectors[i], ref, small_sem.at[1 + i]))
     for i, m in parts:
         reads[i, m].wait()
         if i == 0 and m == 0:
@@ -918,9 +965,11 @@
     for arrived, copy in zip(there, back):
         arrived.wait()
         copy.start()
+    for copy in given:
+        copy.start()
     for part in parts:
         writes[part].wait()
-    for copy in back:
+    for copy in back + given:
         copy.wait()
 
 
@@ -945,7 +994,6 @@
     img = rows // PLACES
     slots = n_tensor
     extra = max(n_dp.bit_length() - 4, 1)
-    vmem = pl.BlockSpec(memory_space=pltpu.VMEM)
     hbm = pl.BlockSpec(memory_space=pltpu.HBM)
     V = pltpu.VMEM
     DMA = pltpu.SemaphoreType.DMA
@@ -969,11 +1017,11 @@
         V((5, G, 8, LANES), f32),
         V((slots, 2, D, D), bf16),
         V((slots, 2, D // 2, D), bf16),
-        V((slots - 1, 2, D // 4, D), bf16),
-        V((slots - 1, 2, D // 8, D), bf16),
+        V((slots - 1, 2, 2, D // 8, D), bf16),
+        V((slots - 1, 2, 2, D // 16, D), bf16),
         V((2, D // 2, D), bf16),
-        V((slots - 2, 2, D // 8, D), bf16),
-        V((extra, 2, D // 8 if n_dp > 8 else 16, D), bf16),
+        V((slots - 2, 2, 2, D // 16, D), bf16),
+        V((extra, 2, 2, D // 16 if n_dp > 8 else 16, D), bf16),
         V((2, D // 2, D), bf16),
         V((SMALL, D), f32),
         V((7, 8, D), f32),
@@ -982,14 +1030,14 @@
         V((SMALL, D), f32),
         DMA((12,)),
         DMA((1 + G,)),
-        DMA((slots, 2, 4)),
-        DMA((slots, 2, 4)),
+        DMA((slots, 2, 8)),
+        DMA((slots, 2, 8)),
         DMA((slots,)),
         DMA((slots,)),
-        DMA((slots, 2, 6)),
-        DMA((slots, 2, 6)),
-        DMA((extra, 2)),
-        DMA((extra, 2)),
+        DMA((slots, 2, 12)),
+        DMA((slots, 2, 12)),
+        DMA((extra, 2, 2)),
+        DMA((extra, 2, 2)),
         DMA((4, 8)),
         DMA((4, 8)),
     ]
@@ -1035,17 +1083,21 @@
             jax.ShapeDtypeStruct((TAPS, D), f32),
             vec, vec, vec, square, vec, square, vec, vec,
         ],
-        in_specs=[hbm, hbm, hbm, hbm, vmem],
-        out_specs=[hbm, hbm, vmem, vmem, vmem, vmem, hbm, vmem, hbm, vmem, vmem],
+        in_specs=[hbm] * 5,
+        out_specs=[hbm] * 11,
         scratch_shapes=[
             V((2, D, D), bf16),
             V((2, D, D), f32),
             V((rows, D), f32),
             V((rows, D), bf16),
+            V((SMALL, D), f32),
+            V((TAPS, D), f32),
+            *[V((D,), f32) for _ in range(6)],
             DMA((4,)),
             DMA((4,)),
             DMA((2, 3)),
             DMA((2, 3)),
+            DMA((7,)),
         ],
         compiler_params=pltpu.CompilerParams(vmem_limit_bytes=60 << 20),
     )(block_out, input_grad, gr, ge, small)

time: 120 us -> 115 us (0.958)
  Pallas kernels: 119 us -> 114 us
    pallas_call x1, Pallas kernels: 111 us -> 107 us  [per_device(): pl.pallas_call(functools.partial(kernel, n_dp, n_tensor), out_shape=[jax....]
where the time goes in v4:
time: 115 us; the launch traced here: 114 us
  Pallas kernels  114 us (99%)
    pallas_call x1, Pallas kernels, per_device(): pl.pallas_call(functools.partial(kernel, n_dp, n_tensor), out_shape=[jax....  107 us
    pallas_call x1, Pallas kernels, per_device(): pl.pallas_call(hand_over, out_shape=[jax.ShapeDtypeStruct((rows, D), bf16...  7.02 us

profile of v4, /device:TPU:0, one launch (start us, length us, event | category | flops | bytes accessed | tf_op | source)
XLA Modules:
  0.0 114.5 jit_solution(15281392473185246684)
XLA Ops:
  0.6 106.6 %shard_map.203 = (bf16[800,768]{1,0:T(8,128)(2,1)}, f32[800,768]{1,0:T(8,128)}, bf16[768,768]{1,0:T(8,128)(2,1)}, bf16[768,768]{1,0:T(8,128)(2,1)}, f32[64,768]{1,0:T(8,128)}) custom-call(bf16[800,768]{1,0:T(8,128)(2,1)} %pix_hbm.1, s32[8]{0:T(128)} %side_hbm.1, bf16[800,768]{1,0:T(8,128)(2,1)} %cot_hbm.1, bf16[49,768]{1,0:T(8,128)(2,1)} %taps_hbm.1, ...), custom_call_target="tpu_custom_call" | custom-call | flops 22649241600 | bytes 12288000 | tf_op jit(solution)/shard_map/pallas_call | solution.py:1044
  107.2 7.0 %shard_map.204 = (bf16[800,768]{1,0:T(8,128)(2,1)}, f32[800,768]{1,0:T(8,128)}, f32[49,768]{1,0:T(8,128)}, f32[768]{0:T(1024)}, f32[768]{0:T(1024)}, /*index=5*/...) custom-call(bf16[800,768]{1,0:T(8,128)(2,1)} %get-tuple-element.16.o, ...), custom_call_target="tpu_custom_call" | custom-call | tf_op jit(solution)/shard_map/pallas_call | solution.py:1078

commit v5 on v4

--- a/solution.py
+++ b/solution.py
@@ -26,12 +26,13 @@
     "h:0:1", "W2.2.0", "W1.3.1", "W3.1.1", "h:0:2", "h:0:3", "h:1:0", "h:1:1", "h:1:2", "h:1:3",
     "gr:1:0", "G0.1.0", "W2.3.0", "W3.2.1", "gr:1:1", "W3.2.0", "G1.1.0", "W2.3.1", "gr:0:0",
     "h:2:0", "h:2:1", "W3.3.0", "h:2:2", "G0.1.1", "h:2:3", "gr:2:1", "W3.3.1", "gr:2:0", "G1.1.1",
-    "G0.2.0", "h:3:0", "h:3:1", "G0.2.1", "G1.2.0", "h:3:2", "h:3:3", "gr:3:0", "G1.2.1", "ncot",
-    "G0.3.0", "G2.2.0", "G0.0.0", "gr:3:1", "G2.2.1", "gr:0:1", "G0.3.1", "G1.3.0", "lnb",
-    "G1.0.0", "G3.2.1", "G3.2.0", "branch", "G2.3.0", "bout", "G0.0.1", "G2.0.0", "G1.3.1", "kg:0",
-    "G3.3.0", "G1.0.1", "kg:1", "kg:2", "kg:3", "G2.3.1", "kg:4", "kg:5", "A0.0", "small", "S0",
-    "G2.0.1", "G3.3.1", "convb:0", "A1.0", "convb:1", "S1", "A0.1", "convb:2", "convb:3", "A1.1",
-    "S2", "convb:4", "A2.0", "convb:5", "S3", "A2.1",
+    "G0.2.0", "h:3:0", "h:3:1", "G0.2.1", "G1.2.0", "h:3:2", "h:3:3", "gr:3:0", "G1.2.1", "ncot:0",
+    "ncot:1", "ncot:2", "G0.3.0", "G2.2.0", "G0.0.0", "gr:3:1", "G2.2.1", "gr:0:1", "G0.3.1",
+    "G1.3.0", "lnb", "G1.0.0", "G3.2.1", "G3.2.0", "branch:0", "branch:1", "branch:2", "G2.3.0",
+    "bout:0", "bout:1", "G0.0.1", "G2.0.0", "G1.3.1", "kg:0", "G3.3.0", "G1.0.1", "kg:1", "kg:2",
+    "kg:3", "G2.3.1", "kg:4", "kg:5", "A0.0", "small", "S0", "G2.0.1", "G3.3.1", "convb:0", "A1.0",
+    "convb:1", "S1", "A0.1", "convb:2", "convb:3", "A1.1", "S2", "convb:4", "A2.0", "convb:5",
+    "S3", "A2.1",
 )
 
 
@@ -686,25 +687,23 @@
             else:
                 GS[s, 1, :, cols] = dot_rows(NM[...], HC[s, :, cols]).astype(bf16)
 
-    def back_to_normed():
-        for n in range(D // BLOCK):
-            cols = slice(n * BLOCK, (n + 1) * BLOCK)
-            total = dot_t(HC[0], WE[0, cols, :])
-            for s in range(1, SLOTS):
-                total = total + dot_t(HC[s], WE[s, cols, :])
-            NC[2 * n] = total[:, :LANES]
-            NC[2 * n + 1] = total[:, LANES:]
-
-    def to_branch():
-        for n in range(D // BLOCK):
-            cols = slice(n * BLOCK, (n + 1) * BLOCK)
-            total = dot(ACT[0], WR[0, :, cols])
-            for s in range(1, SLOTS):
-                total = total + dot(ACT[s], WR[s, :, cols])
-            XH[2 * n] = total[:, :LANES]
-            XH[2 * n + 1] = total[:, LANES:]
-
-    def block_output():
+    def back_to_normed(n):
+        cols = slice(n * BLOCK, (n + 1) * BLOCK)
+        total = dot_t(HC[0], WE[0, cols, :])
+        for s in range(1, SLOTS):
+            total = total + dot_t(HC[s], WE[s, cols, :])
+        NC[2 * n] = total[:, :LANES]
+        NC[2 * n + 1] = total[:, LANES:]
+
+    def to_branch(n):
+        cols = slice(n * BLOCK, (n + 1) * BLOCK)
+        total = dot(ACT[0], WR[0, :, cols])
+        for s in range(1, SLOTS):
+            total = total + dot(ACT[s], WR[s, :, cols])
+        XH[2 * n] = total[:, :LANES]
+        XH[2 * n + 1] = total[:, LANES:]
+
+    def block_output(part):
         scale = vector(scale_ref)
         shift = vector(rb_ref)
 
@@ -722,9 +721,12 @@
             return tuple(sums)
 
         zero = jnp.zeros((IMG, LANES), f32)
-        sums = lax.fori_loop(0, PLACES // 2, body, (zero,) * G)
+        n = PLACES // 4
+        sums = lax.fori_loop(part * n, part * n + n, body, (zero,) * G)
         for g in range(G):
-            ACC[4, g] = sums[g]
+            ACC[4, g] = sums[g] if part == 0 else ACC[4, g] + sums[g]
+        if part == 0:
+            return
 
         def narrow(i, c):
             rows = pl.ds(pl.multiple_of(i * 80, 16), 80)
@@ -803,9 +805,10 @@
         "convb": lambda between: conv(NC, None, None, True, finish_input, between),
     }
 
-    def start_output():
-        block_output()
-        pltpu.make_async_copy(NM, out_hbm, out_sem.at[0]).start()
+    def start_output(part):
+        block_output(part)
+        if part == 1:
+            pltpu.make_async_copy(NM, out_hbm, out_sem.at[0]).start()
 
     def pixels_in():
         spread(NM)
@@ -847,7 +850,7 @@
                 "branch": to_branch,
                 "bout": start_output,
                 "small": small_sums,
-            }[kind]()
+            }[kind](*where)
 
     at = 0
     while at < len(PLAN):
@@ -936,9 +939,27 @@
         for i, m in parts
     }
     load = pltpu.make_async_copy(small, sums, small_sem.at[0])
+    for part in parts[:2]:
+        reads[part].start()
+    for copy in there:
+        copy.start()
     load.start()
-    for part in parts:
+    for part in parts[2:]:
         reads[part].start()
+    for i, m in parts:
+        reads[i, m].wait()
+        def widen(k, c):
+            at = pl.ds(pl.multiple_of(i * third + k * 32, 32), 32)
+            wide[m, at, :] = narrow[m, at, :].astype(f32)
+            return c
+
+        lax.fori_loop(0, third // 32, widen, 0)
+        writes[i, m].start()
+        if m == 1:
+            for k in range(len(there)):
+                if k * 3 // len(there) == i:
+                    there[k].wait()
+                    back[k].start()
     load.wait()
     taps[...] = sums[:TAPS, :]
     own = ROW_EXPAND + lax.axis_index("tensor")
@@ -949,22 +970,6 @@
     )):
         vectors[i][...] = sums[pl.ds(row, 1), :].reshape(D)
         given.append(pltpu.make_async_copy(vectors[i], ref, small_sem.at[1 + i]))
-    for i, m in parts:
-        reads[i, m].wait()
-        if i == 0 and m == 0:
-            for copy in there:
-                copy.start()
-
-        def widen(k, c):
-            at = pl.ds(pl.multiple_of(i * third + k * 32, 32), 32)
-            wide[m, at, :] = narrow[m, at, :].astype(f32)
-            return c
-
-        lax.fori_loop(0, third // 32, widen, 0)
-        writes[i, m].start()
-    for arrived, copy in zip(there, back):
-        arrived.wait()
-        copy.start()
     for copy in given:
         copy.start()
     for part in parts:

time: 115 us -> 114 us (level)
  no operation moved by 1% of the time
where the time goes in v5:
time: 114 us
  Pallas kernels  113 us (99%)
    pallas_call x1, Pallas kernels, per_device(): pl.pallas_call(functools.partial(kernel, n_dp, n_tensor), out_shape=[jax....  107 us
    pallas_call x1, Pallas kernels, per_device(): pl.pallas_call(hand_over, out_shape=[jax.ShapeDtypeStruct((rows, D), bf16...  6.13 us

profile of v5, /device:TPU:0, one launch (start us, length us, event | category | flops | bytes accessed | tf_op | source)
XLA Modules:
  0.0 113.6 jit_solution(9767807957289313907)
XLA Ops:
  0.6 106.6 %shard_map.203 = (bf16[800,768]{1,0:T(8,128)(2,1)}, f32[800,768]{1,0:T(8,128)}, bf16[768,768]{1,0:T(8,128)(2,1)}, bf16[768,768]{1,0:T(8,128)(2,1)}, f32[64,768]{1,0:T(8,128)}) custom-call(bf16[800,768]{1,0:T(8,128)(2,1)} %pix_hbm.1, s32[8]{0:T(128)} %side_hbm.1, bf16[800,768]{1,0:T(8,128)(2,1)} %cot_hbm.1, bf16[49,768]{1,0:T(8,128)(2,1)} %taps_hbm.1, ...), custom_call_target="tpu_custom_call" | custom-call | flops 22649241600 | bytes 12288000 | tf_op jit(solution)/shard_map/pallas_call | solution.py:1049
  107.2 6.1 %shard_map.204 = (bf16[800,768]{1,0:T(8,128)(2,1)}, f32[800,768]{1,0:T(8,128)}, f32[49,768]{1,0:T(8,128)}, f32[768]{0:T(1024)}, f32[768]{0:T(1024)}, /*index=5*/...) custom-call(bf16[800,768]{1,0:T(8,128)(2,1)} %get-tuple-element.16.o, ...), custom_call_target="tpu_custom_call" | custom-call | tf_op jit(solution)/shard_map/pallas_call | solution.py:1083

commit v6 on v5

--- a/solution.py
+++ b/solution.py
@@ -26,10 +26,10 @@
     "h:0:1", "W2.2.0", "W1.3.1", "W3.1.1", "h:0:2", "h:0:3", "h:1:0", "h:1:1", "h:1:2", "h:1:3",
     "gr:1:0", "G0.1.0", "W2.3.0", "W3.2.1", "gr:1:1", "W3.2.0", "G1.1.0", "W2.3.1", "gr:0:0",
     "h:2:0", "h:2:1", "W3.3.0", "h:2:2", "G0.1.1", "h:2:3", "gr:2:1", "W3.3.1", "gr:2:0", "G1.1.1",
-    "G0.2.0", "h:3:0", "h:3:1", "G0.2.1", "G1.2.0", "h:3:2", "h:3:3", "gr:3:0", "G1.2.1", "ncot:0",
-    "ncot:1", "ncot:2", "G0.3.0", "G2.2.0", "G0.0.0", "gr:3:1", "G2.2.1", "gr:0:1", "G0.3.1",
-    "G1.3.0", "lnb", "G1.0.0", "G3.2.1", "G3.2.0", "branch:0", "branch:1", "branch:2", "G2.3.0",
-    "bout:0", "bout:1", "G0.0.1", "G2.0.0", "G1.3.1", "kg:0", "G3.3.0", "G1.0.1", "kg:1", "kg:2",
+    "G0.2.0", "h:3:0", "h:3:1", "G0.2.1", "G1.2.0", "h:3:2", "h:3:3", "gr:3:0", "G0.3.0", "G1.2.1",
+    "gr:3:1", "G0.3.1", "ncot:0", "ncot:1", "G2.2.0", "ncot:2", "G0.0.0", "G2.2.1", "gr:0:1",
+    "G0.0.1", "G1.3.0", "lnb", "G1.0.0", "G3.2.1", "G3.2.0", "branch:0", "branch:1", "branch:2",
+    "G2.3.0", "bout:0", "bout:1", "G2.0.0", "G1.3.1", "kg:0", "G3.3.0", "G1.0.1", "kg:1", "kg:2",
     "kg:3", "G2.3.1", "kg:4", "kg:5", "A0.0", "small", "S0", "G2.0.1", "G3.3.1", "convb:0", "A1.0",
     "convb:1", "S1", "A0.1", "convb:2", "convb:3", "A1.1", "S2", "convb:4", "A2.0", "convb:5",
     "S3", "A2.1",
@@ -939,13 +939,15 @@
         for i, m in parts
     }
     load = pltpu.make_async_copy(small, sums, small_sem.at[0])
+    load.start()
     for part in parts[:2]:
         reads[part].start()
-    for copy in there:
+    for copy in there[:2]:
         copy.start()
-    load.start()
     for part in parts[2:]:
         reads[part].start()
+    for copy in there[2:]:
+        copy.start()
     for i, m in parts:
         reads[i, m].wait()
         def widen(k, c):

time: 114 us -> 114 us (level)
  no operation moved by 1% of the time
where the time goes in v6:
time: 114 us; the launch traced here: 113 us
  Pallas kernels  113 us (99%)
    pallas_call x1, Pallas kernels, per_device(): pl.pallas_call(functools.partial(kernel, n_dp, n_tensor), out_shape=[jax....  107 us
    pallas_call x1, Pallas kernels, per_device(): pl.pallas_call(hand_over, out_shape=[jax.ShapeDtypeStruct((rows, D), bf16...  5.76 us

profile of v6, /device:TPU:0, one launch (start us, length us, event | category | flops | bytes accessed | tf_op | source)
XLA Modules:
  0.0 113.4 jit_solution(11804189783573080835)
XLA Ops:
  0.6 106.8 %shard_map.203 = (bf16[800,768]{1,0:T(8,128)(2,1)}, f32[800,768]{1,0:T(8,128)}, bf16[768,768]{1,0:T(8,128)(2,1)}, bf16[768,768]{1,0:T(8,128)(2,1)}, f32[64,768]{1,0:T(8,128)}) custom-call(bf16[800,768]{1,0:T(8,128)(2,1)} %pix_hbm.1, s32[8]{0:T(128)} %side_hbm.1, bf16[800,768]{1,0:T(8,128)(2,1)} %cot_hbm.1, bf16[49,768]{1,0:T(8,128)(2,1)} %taps_hbm.1, ...), custom_call_target="tpu_custom_call" | custom-call | flops 22649241600 | bytes 12288000 | tf_op jit(solution)/shard_map/pallas_call | solution.py:1051
  107.4 5.8 %shard_map.204 = (bf16[800,768]{1,0:T(8,128)(2,1)}, f32[800,768]{1,0:T(8,128)}, f32[49,768]{1,0:T(8,128)}, f32[768]{0:T(1024)}, f32[768]{0:T(1024)}, /*index=5*/...) custom-call(bf16[800,768]{1,0:T(8,128)(2,1)} %get-tuple-element.16.o, ...), custom_call_target="tpu_custom_call" | custom-call | tf_op jit(solution)/shard_map/pallas_call | solution.py:1085
